TPU v7x, 32 devices: a whole 2x2x4 slice. The times are simulated.
32 devices in a mesh: st: 8 (over z, x), ta: 4 (over y, core).
Axes of the slice: x: 2, y: 2, z: 4, core: 2. Of those that a mesh axis runs over, the one named last changes fastest.
Arguments:
- samples: bfloat16 [128, 128, 8192], P('st', 'ta'), may hold values from -6 to 6
- coefficients: float32 [16, 8192], replicated, may hold values from -1.5 to 1.5
Outputs:
- visibilities: bfloat16 [32, 2, 128, 128], P(('st', 'ta'))
All inputs are finite; a program needn't handle non-finite values.
Results may differ from a plain program's by a relative error of at most 0.0056.
Values may be sent and summed in bfloat16 or wider, within the bound.
No kernel may reach another device: no remote copies, remote signals or barrier semaphores. Data moves between devices by JAX's collectives and lax.ppermute only.
A program may use at most 128 MiB of HBM per device.

v0:
```python
import math

import jax
import jax.numpy as jnp
from jax import lax
from jax.sharding import PartitionSpec as P

CH0 = 1024


def shifted(block, axis, distance):
    devices = range(lax.axis_size(axis))
    route = [(i - distance, i) for i in devices if i - distance in devices]
    return lax.ppermute(block, axis, route)


def phase_table(frame_len, channel_count, first_channel):
    positions = jnp.arange(frame_len, dtype=jnp.int32)[:, None]
    channels = (first_channel + jnp.arange(channel_count, dtype=jnp.int32))[None, :]
    phases = positions * channels % frame_len
    angles = 2.0 * math.pi / frame_len * phases.astype(jnp.float32)
    scale = jnp.float32(frame_len ** (-0.5))
    stacked = jnp.stack([jnp.cos(angles) * scale, -jnp.sin(angles) * scale], axis=2)
    return stacked.reshape(frame_len, 2 * channel_count)


def filter_frames(extended, coefficients, frame_count):
    total_sum = jnp.zeros((extended.shape[0], frame_count, extended.shape[2]), jnp.float32)
    for tap_index in range(coefficients.shape[0]):
        window = extended[:, tap_index : tap_index + frame_count, :].astype(jnp.float32)
        total_sum = total_sum + coefficients[tap_index][None, None, :] * window
    return total_sum


def channelize_rows(filtered, table):
    return jnp.einsum("ifk,kc->cif", filtered, table, precision=lax.Precision.HIGHEST)


def on_device(samples, coefficients):
    tap_count = coefficients.shape[0]
    frame_len = samples.shape[2]
    frame_count = samples.shape[1]
    st_count = lax.axis_size("st")
    ta_count = lax.axis_size("ta")
    channel_count = st_count * ta_count
    table = phase_table(frame_len, channel_count, CH0)
    head_frames = samples[:, : tap_count - 1, :]
    arrived = shifted(head_frames, "ta", -1)
    extended = jnp.concatenate([samples, arrived], 1)
    spectrum = channelize_rows(filter_frames(extended, coefficients, frame_count), table)
    spectra = spectrum.astype(jnp.bfloat16)
    turned = lax.all_to_all(
        lax.all_to_all(spectra, "st", split_axis=0, concat_axis=1, tiled=True),
        "ta",
        split_axis=0,
        concat_axis=2,
        tiled=True,
    )
    real_part = turned[0]
    imag_part = turned[1]
    all_inputs = real_part.shape[0]
    left_rows = jnp.concatenate(
        [jnp.concatenate([real_part, imag_part], 1), jnp.concatenate([imag_part, -real_part], 1)], 0
    )
    right_rows = jnp.concatenate([real_part, imag_part], 1)
    product = lax.dot_general(
        left_rows, right_rows, (((1,), (1,)), ((), ())), preferred_element_type=jnp.float32
    )
    averaged = product / jnp.float32(real_part.shape[1])
    return averaged.reshape(1, 2, all_inputs, all_inputs).astype(jnp.bfloat16)


def solution(mesh):
    return jax.shard_map(
        on_device,
        mesh=mesh,
        in_specs=(P("st", "ta", None), P()),
        out_specs=P(("st", "ta"), None, None, None),
        check_vma=False,
    )
```

profile of v0, /device:TPU:0, one launch (start us, length us, event | category | flops | bytes accessed | tf_op | source)
XLA Modules:
  0.0 158.1 jit_solution(3440681869598262412)
XLA Ops:
  0.0 2.5 %slice.106 = bf16[16,15,8192]{2,1,0:T(8,128)(2,1)S(1)} slice(bf16[16,32,8192]{2,1,0:T(8,128)(2,1)} %param.2), slice={[0:16], [0:15], [0:8192]} | slice | bytes 7864320 | tf_op jit(solution)/shard_map/slice | solution.py:47
  2.5 4.2 %copy.27 = bf16[16,15,8192]{2,0,1:T(8,128)(2,1)} copy(bf16[16,15,8192]{2,1,0:T(8,128)(2,1)S(1)} %slice.106) | data formatting | bytes 7864320
  6.6 1.5 collective-permute-start
  8.1 4.2 %cosine_multiply_fusion = (f32[8192,32,1]{0,1,2:T(8,128)S(1)}, f32[8192,32,1]{0,1,2:T(8,128)S(1)}) fusion(s32[32]{0:T(128)S(1)} %iota_add_fusion), kind=kLoop, calls=%fused_computation.91 | loop fusion | flops 4456448 | bytes 2097280 | tf_op jit(solution)/shard_map/mul | solution.py:23
  12.3 0.2 pad_maximum_fusion
  12.5 0.0 copy-start.1
  12.5 1.6 %copy.21 = f32[8192,32,2]{0,2,1:T(2,128)S(1)} copy(f32[8192,32,2]{0,1,2:T(8,128)S(1)} %pad_maximum_fusion) | data formatting | bytes 4194304 | tf_op jit(solution)/shard_map/stack | solution.py:23
  14.1 2.5 %reshape.148 = f32[8192,64,1]{0,1,2:T(8,128)} reshape(f32[8192,32,2]{0,2,1:T(2,128)S(1)} %copy.21) | data formatting | bytes 4194304 | tf_op jit(solution)/shard_map/reshape | solution.py:24
  16.6 0.0 copy-start
  16.6 7.8 %constant_dynamic-update-slice_fusion = bf16[16,47,8192]{2,1,0:T(8,128)(2,1)} fusion(bf16[16,32,8192]{2,1,0:T(8,128)(2,1)} %param.2), kind=kLoop, calls=%fused_computation.105 | loop fusion | bytes 16777216
  24.4 0.0 copy-done.1
  24.4 0.5 fusion.100
  24.9 0.0 collective-permute-done
  24.9 6.2 %copy_dynamic-update-slice_fusion = bf16[16,47,8192]{2,1,0:T(8,128)(2,1)} fusion(bf16[16,47,8192]{2,1,0:T(8,128)(2,1)} %constant_dynamic-update-slice_fusion, bf16[16,15,8192]{2,0,1:T(8,128)(2,1)} %collective-permute-done), kind=kLoop, calls=%fused_computation.79 | loop fusion | bytes 8126464 | tf_op jit(solution)/shard_map/concatenate | solution.py:49
  31.1 0.0 copy-done
  31.1 77.4 %fusion.79 = bf16[64,16,32]{0,2,1:T(8,128)(2,1)S(1)} fusion(f32[8192,64,1]{0,1,2:T(8,128)S(1)} %copy-done, bf16[16,32,8192]{2,1,0:T(8,128)(2,1)} %param.2, bf16[16,47,8192]{2,1,0:T(8,128)(2,1)} %copy_dynamic-update-slice_fusion, f32[8192]{0:T(1024)S(1)} %bitcast.49, f32[8192]{0:T(1024)S(1)} %bitcast.50, f32[8192]{0:T(1024)S(1)} %bitcast.36, ...), kind=kOutput, calls=%fused_computation.84 | convolution fusion | flops 3418390528 | bytes 136904704 | tf_op jit(solution)/shard_map/ifk,kc->cif/dot_general | solution.py:36
  108.5 0.3 copy.24
  108.8 0.3 reshape.150
  109.1 14.0 %all_to_all.33 = bf16[8,2,2048]{2,1,0:T(2,128)(2,1)S(1)} all-to-all(bf16[8,2,2048]{2,1,0:T(2,128)(2,1)S(1)} %reshape.150), channel_id=1, replica_groups=mesh['st'=8,'ta'=4] {'st'}, dimensions={0} | all-to-all | bytes 131072 | tf_op jit(solution)/shard_map/all_to_all | solution.py:53
  123.0 0.2 reshape.151
  123.2 0.1 copy.26
  123.4 33.9 %all_to_all.34 = bf16[8,128,32]{1,2,0:T(8,128)(2,1)S(1)} all-to-all(bf16[8,128,32]{1,2,0:T(8,128)(2,1)S(1)} %copy.26), channel_id=1, replica_groups=mesh['st'=8,'ta'=4] {'ta'}, dimensions={0} | all-to-all | bytes 131072 | tf_op jit(solution)/shard_map/all_to_all | solution.py:52
  157.3 0.9 fusion.82
  (4 shorter events, 0.0 us)
Async XLA Ops:
  6.6 18.2 %collective-permute-start = (bf16[16,15,8192]{2,0,1:T(8,128)(2,1)}, bf16[16,15,8192]{2,0,1:T(8,128)(2,1)}, u32[]{:S(2)}, u32[]{:S(2)}) collective-permute-start(bf16[16,15,8192]{2,0,1:T(8,128)(2,1)} %copy.27), channel_id=1, source_target_pairs={{1,0},{2,1},{3,2},{5,4},{6,5},{7,6},{9,8},{10,9},{11,10},{13,12},{... | collective-permute-start | bytes 11796488 | tf_op jit(solution)/shard_map/ppermute | solution.py:14
  12.5 11.9 %copy-start.1 = (f32[16,8192]{1,0:T(8,128)S(1)}, f32[16,8192]{1,0:T(8,128)}, u32[]{:S(2)}) copy-start(f32[16,8192]{1,0:T(8,128)} %param.3) | copy-start | bytes 1572868
  16.6 14.5 %copy-start = (f32[8192,64,1]{0,1,2:T(8,128)S(1)}, f32[8192,64,1]{0,1,2:T(8,128)}, u32[]{:S(2)}) copy-start(f32[8192,64,1]{0,1,2:T(8,128)} %reshape.148) | copy-start | bytes 6291460
where the time goes:
time: 158 us
  matrix products  78.3 us (50%)
  blocking collectives  47.9 us (30%)
  local copies, waits for them, and re-layouts  26.1 us (17%)
  other arithmetic  4.38 us (3%)
    dot_general x1, matrix products, channelize_rows(): jnp.einsum('ifk,kc->cif', filtered, table, precision=lax.Precision.HIGHEST)  77.4 us
    all_to_all x1, blocking collectives, on_device(): lax.all_to_all(lax.all_to_all(spectra, 'st', split_axis=0, concat_axis=1,...  33.9 us
    all_to_all x1, blocking collectives, on_device(): lax.all_to_all(spectra, 'st', split_axis=0, concat_axis=1, tiled=True)  14 us
    unnamed x8, local copies, waits for them, and re-layouts  12.4 us
    concatenate x1, local copies, waits for them, and re-layouts, on_device(): extended = jnp.concatenate([samples, arrived], 1)  6.22 us
    mul x1, other arithmetic, phase_table(): jnp.cos(angles) * scale  4.21 us
  transfers between devices with their start and end apart: 1, of which 0 were waited for; matrix products, arithmetic and copies ran while one was open for 11% of the time, Pallas kernels for 0%

commit v1 on v0

v1 whole, which is shorter than its diff:
```python
import functools
import math

import jax
import jax.numpy as jnp
import numpy as np
from jax import lax
from jax.experimental import pallas as pl
from jax.experimental.pallas import tpu as pltpu
from jax.sharding import PartitionSpec as P

CH0 = 1024
LANES = 128
CHANNEL_BLOCK = 32
K_BLOCK = 1024
NT = (((1,), (1,)), ((), ()))


def phase_table(frame_len, channel_count, first_channel):
    channels = first_channel + np.arange(channel_count, dtype=np.int64)
    phases = (channels[:, None] * np.arange(frame_len, dtype=np.int64)[None, :]) % frame_len
    angles = 2.0 * math.pi / frame_len * phases
    parts = np.stack([np.cos(angles), -np.sin(angles)]) * frame_len**-0.5
    blocks = parts.reshape(2, channel_count // CHANNEL_BLOCK, CHANNEL_BLOCK, frame_len)
    return blocks.transpose(1, 0, 2, 3).reshape(-1, 2 * CHANNEL_BLOCK, frame_len).astype(np.float32)


def channelize_kernel(frame_count, x_ref, coef_ref, table_ref, out_ref, folded, total, turned):
    step = pl.program_id(1)
    taps = coef_ref.shape[0]
    rows = table_ref.shape[1]
    table = table_ref[0]
    for tap in range(taps):
        folded[tap * rows : (tap + 1) * rows, :] = (table * coef_ref[tap : tap + 1, :]).astype(jnp.bfloat16)
    product = lax.dot_general(folded[...], x_ref[...], NT, preferred_element_type=jnp.float32)

    @pl.when(step == 0)
    def _():
        total[...] = product

    @pl.when(step > 0)
    def _():
        total[...] += product

    @pl.when(step == pl.num_programs(1) - 1)
    def _():
        half = rows // 2
        groups = total.shape[1] // LANES
        slots = 4 * groups
        frame = lax.broadcasted_iota(jnp.int32, (rows, LANES), 1) % frame_count
        for group in range(groups):
            lanes = slice(group * LANES, (group + 1) * LANES)
            both = total[0:rows, lanes]
            own = both
            for tap in range(1, taps):
                moved = pltpu.roll(total[tap * rows : (tap + 1) * rows, lanes], LANES - tap, 1)
                both = both + moved
                own = own + jnp.where(frame < frame_count - tap, moved, 0.0)
            ahead = pltpu.roll(both - own, frame_count, 1)
            for part in range(2):
                turned[pl.ds(part * groups + group, half, stride=slots), :] = own[part * half : (part + 1) * half]
                turned[pl.ds((2 + part) * groups + group, half, stride=slots), :] = ahead[
                    part * half : (part + 1) * half
                ]
        out_ref[...] = turned[...].astype(jnp.bfloat16).reshape(out_ref.shape)


def channelize(samples, coefficients, channel_count):
    inputs, frame_count, frame_len = samples.shape
    taps = coefficients.shape[0]
    rows = 2 * CHANNEL_BLOCK
    columns = inputs * frame_count
    blocks = channel_count // CHANNEL_BLOCK
    slots = 4 * columns // LANES
    k_block = min(K_BLOCK, frame_len)
    table = jnp.asarray(phase_table(frame_len, channel_count, CH0))
    return pl.pallas_call(
        functools.partial(channelize_kernel, frame_count),
        grid=(blocks, frame_len // k_block),
        in_specs=[
            pl.BlockSpec((columns, k_block), lambda b, k: (0, k)),
            pl.BlockSpec((taps, k_block), lambda b, k: (0, k)),
            pl.BlockSpec((1, rows, k_block), lambda b, k: (b, 0, k)),
        ],
        out_specs=pl.BlockSpec((CHANNEL_BLOCK, slots, LANES), lambda b, k: (b, 0, 0)),
        out_shape=jax.ShapeDtypeStruct((channel_count, slots, LANES), jnp.bfloat16),
        scratch_shapes=[
            pltpu.VMEM((taps * rows, k_block), jnp.bfloat16),
            pltpu.VMEM((taps * rows, columns), jnp.float32),
            pltpu.VMEM((CHANNEL_BLOCK * slots, LANES), jnp.float32),
        ],
        compiler_params=pltpu.CompilerParams(
            dimension_semantics=("arbitrary", "arbitrary"), vmem_limit_bytes=48 * 1024 * 1024
        ),
        cost_estimate=pl.CostEstimate(
            flops=2 * channel_count * 2 * taps * columns * frame_len,
            bytes_accessed=2 * columns * frame_len,
            transcendentals=0,
        ),
        name="channelize",
    )(samples.reshape(columns, frame_len), coefficients, table)


def correlate_kernel(frame_count, st_count, ta_count, in_ref, out_ref, spectra):
    slots = in_ref.shape[1]
    half = slots // 2
    groups = half // 2
    per_row = LANES // frame_count
    all_inputs = st_count * groups * per_row
    position = lax.broadcasted_iota(jnp.int32, (half, LANES), 1) // frame_count

    def station(st, _):
        sums = []
        for ta in range(ta_count):
            block = in_ref[st * ta_count + ta].astype(jnp.float32)
            value = block[:half]
            if ta < ta_count - 1:
                value = value + in_ref[st * ta_count + ta + 1].astype(jnp.float32)[half:]
            sums.append(value)
        for column in range(ta_count * frame_count // LANES):
            for slot in range(per_row):
                result = None
                for place in range(per_row):
                    value = sums[column * per_row + place]
                    shift = ((place - slot) * frame_count) % LANES
                    if shift:
                        value = pltpu.roll(value, shift, 1)
                    result = value if result is None else jnp.where(position == place, value, result)
                for part in range(2):
                    first = part * all_inputs + st * groups * per_row + slot
                    spectra[pl.ds(first, groups, stride=per_row), column * LANES : (column + 1) * LANES] = result[
                        part * groups : (part + 1) * groups
                    ]
        return 0

    if st_count <= 8:
        for st in range(st_count):
            station(st, 0)
    else:
        lax.fori_loop(0, st_count, station, 0)
    real_part = spectra[:all_inputs, :].astype(jnp.bfloat16)
    imag_part = spectra[all_inputs:, :].astype(jnp.bfloat16)
    right = jnp.concatenate([real_part, imag_part], 1)
    left = jnp.concatenate([imag_part, -real_part], 1)
    scale = 1.0 / (ta_count * frame_count)
    for part, rows in enumerate((right, left)):
        product = lax.dot_general(rows, right, NT, preferred_element_type=jnp.float32)
        out_ref[0, part] = (product * scale).astype(jnp.bfloat16)


def correlate(arrived, frame_count, st_count, ta_count, all_inputs):
    return pl.pallas_call(
        functools.partial(correlate_kernel, frame_count, st_count, ta_count),
        in_specs=[pl.BlockSpec(memory_space=pltpu.VMEM)],
        out_specs=pl.BlockSpec(memory_space=pltpu.VMEM),
        out_shape=jax.ShapeDtypeStruct((1, 2, all_inputs, all_inputs), jnp.bfloat16),
        scratch_shapes=[pltpu.VMEM((2 * all_inputs, ta_count * frame_count), jnp.float32)],
        compiler_params=pltpu.CompilerParams(vmem_limit_bytes=48 * 1024 * 1024),
        name="correlate",
    )(arrived)


def on_device(samples, coefficients):
    st_count = lax.axis_size("st")
    ta_count = lax.axis_size("ta")
    inputs, frame_count, _ = samples.shape
    partial = channelize(samples, coefficients, st_count * ta_count)
    arrived = lax.all_to_all(partial, ("st", "ta"), split_axis=0, concat_axis=0, tiled=True)
    return correlate(arrived, frame_count, st_count, ta_count, st_count * inputs)


def solution(mesh):
    return jax.shard_map(
        on_device,
        mesh=mesh,
        in_specs=(P("st", "ta", None), P()),
        out_specs=P(("st", "ta"), None, None, None),
        check_vma=False,
    )
```

time: 158 us -> 33.4 us (0.21)
  matrix products: 78.3 us -> 0 us
  blocking collectives: 47.9 us -> 15.3 us
  local copies, waits for them, and re-layouts: 26.1 us -> 2.63 us
  Pallas kernels: 0 us -> 15.2 us
  other arithmetic: 4.38 us -> 0 us
    dot_general x2 -> x0, matrix products: 78.3 us -> none  [the longest x1 77.4 us: channelize_rows(): jnp.einsum('ifk,kc->cif', filtered, table, precision=lax.Precision.HIGHEST)]
    all_to_all x2 -> x1, blocking collectives: 47.9 us -> 15.3 us  [on_device(): lax.all_to_all(partial, ('st', 'ta'), split_axis=0, concat_axis=0, tiled=...]
    pallas_call x0 -> x2, Pallas kernels: none -> 15.2 us  [the longest x1 14.2 us: channelize(): pl.pallas_call(functools.partial(channelize_kernel, frame_count), grid=(b...]
    unnamed x8 -> x4, local copies, waits for them, and re-layouts: 12.4 us -> 2.63 us
    concatenate x1 -> x0, local copies, waits for them, and re-layouts: 6.22 us -> none  [on_device(): extended = jnp.concatenate([samples, arrived], 1)]
    mul x1 -> x0, other arithmetic: 4.21 us -> none  [phase_table(): jnp.cos(angles) * scale]
    slice x3 -> x0, local copies, waits for them, and re-layouts: 2.93 us -> none  [the longest x1 2.46 us: on_device(): head_frames = samples[:, :tap_count - 1, :]]
    reshape x1 -> x0, local copies, waits for them, and re-layouts: 2.5 us -> none  [phase_table(): return stacked.reshape(frame_len, 2 * channel_count)]
  transfers between devices with their start and end apart: 1 -> 0, of which waited for: 0 -> 0; matrix products, arithmetic and copies ran while one was open for 11% -> 0% of each run, Pallas kernels for 0% -> 0%
where the time goes in v1:
time: 33.4 us; the launch traced here: 33.2 us
  blocking collectives  15.3 us (46%)
  Pallas kernels  15.2 us (46%)
  local copies, waits for them, and re-layouts  2.63 us (8%)
    all_to_all x1, blocking collectives, on_device(): lax.all_to_all(partial, ('st', 'ta'), split_axis=0, concat_axis=0, tiled=...  15.3 us
    pallas_call x1, Pallas kernels, channelize(): pl.pallas_call(functools.partial(channelize_kernel, frame_count), grid=(b...  14.2 us
    unnamed x4, local copies, waits for them, and re-layouts  2.63 us
    pallas_call x1, Pallas kernels, correlate(): pl.pallas_call(functools.partial(correlate_kernel, frame_count, st_count,...  0.97 us

profile of v1, /device:TPU:0, one launch (start us, length us, event | category | flops | bytes accessed | tf_op | source)
XLA Modules:
  0.0 33.2 jit_solution(7140103596577283328)
XLA Ops:
  0.0 0.0 copy-start
  0.0 1.0 %copy-done = f32[16,8192]{1,0:T(8,128)S(1)} copy-done((f32[16,8192]{1,0:T(8,128)S(1)}, f32[16,8192]{1,0:T(8,128)}, u32[]{:S(2)}) %copy-start) | copy-done | bytes 524312
  1.0 0.0 copy-start.1
  1.0 1.6 %copy-done.1 = f32[1,64,8192]{2,1,0:T(8,128)S(1)} copy-done((f32[1,64,8192]{2,1,0:T(8,128)S(1)}, f32[1,64,8192]{2,1,0:T(8,128)}, u32[]{:S(2)}) %copy-start.1) | copy-done | bytes 2097176
  2.6 14.2 %channelize.1 = bf16[32,16,128]{2,1,0:T(8,128)(2,1)S(1)} custom-call(bf16[512,8192]{1,0:T(8,128)(2,1)} %bitcast.1, f32[16,8192]{1,0:T(8,128)S(1)} %copy-done, f32[1,64,8192]{2,1,0:T(8,128)S(1)} %copy-done.1), custom_call_target="tpu_custom_call" | custom-call | flops 8589934592 | bytes 8388608 | tf_op jit(solution)/shard_map/channelize/pallas_call | solution.py:77
  16.8 15.3 %all_to_all.5.in_ref = bf16[32,16,128]{2,1,0:T(8,128)(2,1)S(1)} all-to-all(bf16[32,16,128]{2,1,0:T(8,128)(2,1)S(1)} %channelize.1), channel_id=1, replica_groups=mesh['st'=8,'ta'=4] {'st','ta'}, dimensions={0} | all-to-all | bytes 262144 | tf_op jit(solution)/shard_map/all_to_all | solution.py:168
  32.2 1.0 %correlate.1 = bf16[1,2,128,128]{3,2,1,0:T(8,128)(2,1)} custom-call(bf16[32,16,128]{2,1,0:T(8,128)(2,1)S(1)} %all_to_all.5.in_ref), custom_call_target="tpu_custom_call" | custom-call | tf_op jit(solution)/shard_map/correlate/pallas_call | solution.py:152
Async XLA Ops:
  0.0 1.0 %copy-start = (f32[16,8192]{1,0:T(8,128)S(1)}, f32[16,8192]{1,0:T(8,128)}, u32[]{:S(2)}) copy-start(f32[16,8192]{1,0:T(8,128)} %coef_ref.1) | copy-start | bytes 1572868
  1.0 1.6 %copy-start.1 = (f32[1,64,8192]{2,1,0:T(8,128)S(1)}, f32[1,64,8192]{2,1,0:T(8,128)}, u32[]{:S(2)}) copy-start(f32[1,64,8192]{2,1,0:T(8,128)} %constant.2.clone.table_ref) | copy-start | bytes 6291460

commit v2 on v1

--- a/solution.py
+++ b/solution.py
@@ -12,7 +12,8 @@
 CH0 = 1024
 LANES = 128
 CHANNEL_BLOCK = 32
-K_BLOCK = 1024
+K_BLOCK = 2048
+VMEM_LIMIT = 60 * 1024 * 1024
 NT = (((1,), (1,)), ((), ()))
 
 
@@ -90,7 +91,7 @@
             pltpu.VMEM((CHANNEL_BLOCK * slots, LANES), jnp.float32),
         ],
         compiler_params=pltpu.CompilerParams(
-            dimension_semantics=("arbitrary", "arbitrary"), vmem_limit_bytes=48 * 1024 * 1024
+            dimension_semantics=("arbitrary", "arbitrary"), vmem_limit_bytes=VMEM_LIMIT
         ),
         cost_estimate=pl.CostEstimate(
             flops=2 * channel_count * 2 * taps * columns * frame_len,
@@ -155,7 +156,7 @@
         out_specs=pl.BlockSpec(memory_space=pltpu.VMEM),
         out_shape=jax.ShapeDtypeStruct((1, 2, all_inputs, all_inputs), jnp.bfloat16),
         scratch_shapes=[pltpu.VMEM((2 * all_inputs, ta_count * frame_count), jnp.float32)],
-        compiler_params=pltpu.CompilerParams(vmem_limit_bytes=48 * 1024 * 1024),
+        compiler_params=pltpu.CompilerParams(vmem_limit_bytes=VMEM_LIMIT),
         name="correlate",
     )(arrived)
 

time: 33.4 us -> 31.2 us (0.934)
  local copies, waits for them, and re-layouts: 2.63 us -> 0 us
    unnamed x4 -> x0, local copies, waits for them, and re-layouts: 2.63 us -> none
    pallas_call x1, Pallas kernels: 0.97 us -> 1.87 us  [correlate(): pl.pallas_call(functools.partial(correlate_kernel, frame_count, st_count,...]
    pallas_call x1, Pallas kernels: 14.2 us -> 13.5 us  [channelize(): pl.pallas_call(functools.partial(channelize_kernel, frame_count), grid=(b...]
where the time goes in v2:
time: 31.2 us; the launch traced here: 31 us
  blocking collectives  15.6 us (50%)
  Pallas kernels  15.4 us (49%)
    all_to_all x1, blocking collectives, on_device(): lax.all_to_all(partial, ('st', 'ta'), split_axis=0, concat_axis=0, tiled=...  15.6 us
    pallas_call x1, Pallas kernels, channelize(): pl.pallas_call(functools.partial(channelize_kernel, frame_count), grid=(b...  13.5 us
    pallas_call x1, Pallas kernels, correlate(): pl.pallas_call(functools.partial(correlate_kernel, frame_count, st_count,...  1.87 us

profile of v2, /device:TPU:0, one launch (start us, length us, event | category | flops | bytes accessed | tf_op | source)
XLA Modules:
  0.0 31.0 jit_solution(67578261600177938)
XLA Ops:
  0.0 13.5 %channelize.1 = bf16[32,16,128]{2,1,0:T(8,128)(2,1)} custom-call(bf16[512,8192]{1,0:T(8,128)(2,1)} %bitcast.1, f32[16,8192]{1,0:T(8,128)} %coef_ref.1, f32[1,64,8192]{2,1,0:T(8,128)} %constant.2.clone.table_ref), custom_call_target="tpu_custom_call" | custom-call | flops 8589934592 | bytes 8388608 | tf_op jit(solution)/shard_map/channelize/pallas_call | solution.py:78
  13.5 15.6 %all_to_all.5.in_ref = bf16[32,16,128]{2,1,0:T(8,128)(2,1)} all-to-all(bf16[32,16,128]{2,1,0:T(8,128)(2,1)} %channelize.1), channel_id=1, replica_groups=mesh['st'=8,'ta'=4] {'st','ta'}, dimensions={0} | all-to-all | bytes 262144 | tf_op jit(solution)/shard_map/all_to_all | solution.py:169
  29.2 1.9 %correlate.1 = bf16[1,2,128,128]{3,2,1,0:T(8,128)(2,1)} custom-call(bf16[32,16,128]{2,1,0:T(8,128)(2,1)} %all_to_all.5.in_ref), custom_call_target="tpu_custom_call" | custom-call | tf_op jit(solution)/shard_map/correlate/pallas_call | solution.py:153

commit v3 on v1

--- a/solution.py
+++ b/solution.py
@@ -12,7 +12,7 @@
 CH0 = 1024
 LANES = 128
 CHANNEL_BLOCK = 32
-K_BLOCK = 1024
+VMEM_LIMIT = 24 * 1024 * 1024
 NT = (((1,), (1,)), ((), ()))
 
 
@@ -25,80 +25,51 @@
     return blocks.transpose(1, 0, 2, 3).reshape(-1, 2 * CHANNEL_BLOCK, frame_len).astype(np.float32)
 
 
-def channelize_kernel(frame_count, x_ref, coef_ref, table_ref, out_ref, folded, total, turned):
-    step = pl.program_id(1)
-    taps = coef_ref.shape[0]
-    rows = table_ref.shape[1]
-    table = table_ref[0]
-    for tap in range(taps):
-        folded[tap * rows : (tap + 1) * rows, :] = (table * coef_ref[tap : tap + 1, :]).astype(jnp.bfloat16)
-    product = lax.dot_general(folded[...], x_ref[...], NT, preferred_element_type=jnp.float32)
+def shift_kernel(frame_count, taps, total, out_ref, turned):
+    rows = total.shape[0] // taps
+    half = rows // 2
+    groups = total.shape[1] // LANES
+    slots = 4 * groups
+    frame = lax.broadcasted_iota(jnp.int32, (rows, LANES), 1) % frame_count
+    for group in range(groups):
+        lanes = slice(group * LANES, (group + 1) * LANES)
+        both = total[0:rows, lanes]
+        own = both
+        for tap in range(1, taps):
+            moved = pltpu.roll(total[tap * rows : (tap + 1) * rows, lanes], LANES - tap, 1)
+            both = both + moved
+            own = own + jnp.where(frame < frame_count - tap, moved, 0.0)
+        ahead = pltpu.roll(both - own, frame_count, 1)
+        for part in range(2):
+            turned[pl.ds(part * groups + group, half, stride=slots), :] = own[part * half : (part + 1) * half]
+            turned[pl.ds((2 + part) * groups + group, half, stride=slots), :] = ahead[part * half : (part + 1) * half]
+    out_ref[...] = turned[...].astype(jnp.bfloat16).reshape(out_ref.shape)
 
-    @pl.when(step == 0)
-    def _():
-        total[...] = product
 
-    @pl.when(step > 0)
-    def _():
-        total[...] += product
-
-    @pl.when(step == pl.num_programs(1) - 1)
-    def _():
-        half = rows // 2
-        groups = total.shape[1] // LANES
-        slots = 4 * groups
-        frame = lax.broadcasted_iota(jnp.int32, (rows, LANES), 1) % frame_count
-        for group in range(groups):
-            lanes = slice(group * LANES, (group + 1) * LANES)
-            both = total[0:rows, lanes]
-            own = both
-            for tap in range(1, taps):
-                moved = pltpu.roll(total[tap * rows : (tap + 1) * rows, lanes], LANES - tap, 1)
-                both = both + moved
-                own = own + jnp.where(frame < frame_count - tap, moved, 0.0)
-            ahead = pltpu.roll(both - own, frame_count, 1)
-            for part in range(2):
-                turned[pl.ds(part * groups + group, half, stride=slots), :] = own[part * half : (part + 1) * half]
-                turned[pl.ds((2 + part) * groups + group, half, stride=slots), :] = ahead[
-                    part * half : (part + 1) * half
-                ]
-        out_ref[...] = turned[...].astype(jnp.bfloat16).reshape(out_ref.shape)
+def channelize_block(rows_of_samples, coefficients, table, frame_count):
+    taps = coefficients.shape[0]
+    rows, frame_len = table.shape
+    columns = rows_of_samples.shape[0]
+    slots = 4 * columns // LANES
+    folded = (coefficients[:, None, :] * table[None, :, :]).astype(jnp.bfloat16).reshape(taps * rows, frame_len)
+    total = lax.dot_general(folded, rows_of_samples, NT, preferred_element_type=jnp.float32)
+    return pl.pallas_call(
+        functools.partial(shift_kernel, frame_count, taps),
+        in_specs=[pl.BlockSpec(memory_space=pltpu.VMEM)],
+        out_specs=pl.BlockSpec(memory_space=pltpu.VMEM),
+        out_shape=jax.ShapeDtypeStruct((CHANNEL_BLOCK, slots, LANES), jnp.bfloat16),
+        scratch_shapes=[pltpu.VMEM((CHANNEL_BLOCK * slots, LANES), jnp.float32)],
+        compiler_params=pltpu.CompilerParams(vmem_limit_bytes=VMEM_LIMIT),
+        name="shift",
+    )(total)
 
 
 def channelize(samples, coefficients, channel_count):
     inputs, frame_count, frame_len = samples.shape
-    taps = coefficients.shape[0]
-    rows = 2 * CHANNEL_BLOCK
-    columns = inputs * frame_count
-    blocks = channel_count // CHANNEL_BLOCK
-    slots = 4 * columns // LANES
-    k_block = min(K_BLOCK, frame_len)
+    rows_of_samples = samples.reshape(inputs * frame_count, frame_len)
     table = jnp.asarray(phase_table(frame_len, channel_count, CH0))
-    return pl.pallas_call(
-        functools.partial(channelize_kernel, frame_count),
-        grid=(blocks, frame_len // k_block),
-        in_specs=[
-            pl.BlockSpec((columns, k_block), lambda b, k: (0, k)),
-            pl.BlockSpec((taps, k_block), lambda b, k: (0, k)),
-            pl.BlockSpec((1, rows, k_block), lambda b, k: (b, 0, k)),
-        ],
-        out_specs=pl.BlockSpec((CHANNEL_BLOCK, slots, LANES), lambda b, k: (b, 0, 0)),
-        out_shape=jax.ShapeDtypeStruct((channel_count, slots, LANES), jnp.bfloat16),
-        scratch_shapes=[
-            pltpu.VMEM((taps * rows, k_block), jnp.bfloat16),
-            pltpu.VMEM((taps * rows, columns), jnp.float32),
-            pltpu.VMEM((CHANNEL_BLOCK * slots, LANES), jnp.float32),
-        ],
-        compiler_params=pltpu.CompilerParams(
-            dimension_semantics=("arbitrary", "arbitrary"), vmem_limit_bytes=48 * 1024 * 1024
-        ),
-        cost_estimate=pl.CostEstimate(
-            flops=2 * channel_count * 2 * taps * columns * frame_len,
-            bytes_accessed=2 * columns * frame_len,
-            transcendentals=0,
-        ),
-        name="channelize",
-    )(samples.reshape(columns, frame_len), coefficients, table)
+    blocks = lax.map(lambda part: channelize_block(rows_of_samples, coefficients, part, frame_count), table)
+    return blocks.reshape(channel_count, -1, LANES)
 
 
 def correlate_kernel(frame_count, st_count, ta_count, in_ref, out_ref, spectra):
@@ -155,7 +126,7 @@
         out_specs=pl.BlockSpec(memory_space=pltpu.VMEM),
         out_shape=jax.ShapeDtypeStruct((1, 2, all_inputs, all_inputs), jnp.bfloat16),
         scratch_shapes=[pltpu.VMEM((2 * all_inputs, ta_count * frame_count), jnp.float32)],
-        compiler_params=pltpu.CompilerParams(vmem_limit_bytes=48 * 1024 * 1024),
+        compiler_params=pltpu.CompilerParams(vmem_limit_bytes=32 * 1024 * 1024),
         name="correlate",
     )(arrived)
 

time: 33.4 us -> 39.1 us (1.17)
  matrix products: 0 us -> 14.4 us
  Pallas kernels: 15.2 us -> 1.87 us
  other arithmetic: 0 us -> 7.24 us
  local copies, waits for them, and re-layouts: 2.63 us -> 0 us
    dot_general x0 -> x1, matrix products: none -> 14.4 us  [channelize_block(): lax.dot_general(folded, rows_of_samples, NT, preferred_element_type=jnp.f...]
    pallas_call x1, Pallas kernels: 14.2 us -> 0.9 us  [channelize_block(): pl.pallas_call(functools.partial(shift_kernel, frame_count, taps), in_spe...]
    convert_element_type x0 -> x1, other arithmetic: none -> 7.24 us  [channelize_block(): (coefficients[:, None, :] * table[None, :, :]).astype(jnp.bfloat16)]
    unnamed x4 -> x0, local copies, waits for them, and re-layouts: 2.63 us -> none
where the time goes in v3:
time: 39.1 us; the launch traced here: 38.9 us
  blocking collectives  15.3 us (39%)
  matrix products  14.4 us (37%)
  other arithmetic  7.24 us (19%)
  Pallas kernels  1.87 us (5%)
    all_to_all x1, blocking collectives, on_device(): lax.all_to_all(partial, ('st', 'ta'), split_axis=0, concat_axis=0, tiled=...  15.3 us
    dot_general x1, matrix products, channelize_block(): lax.dot_general(folded, rows_of_samples, NT, preferred_element_type=jnp.f...  14.4 us
    convert_element_type x1, other arithmetic, channelize_block(): (coefficients[:, None, :] * table[None, :, :]).astype(jnp.bfloat16)  7.24 us
    pallas_call x1, Pallas kernels, correlate(): pl.pallas_call(functools.partial(correlate_kernel, frame_count, st_count,...  0.97 us
    pallas_call x1, Pallas kernels, channelize_block(): pl.pallas_call(functools.partial(shift_kernel, frame_count, taps), in_spe...  0.9 us

profile of v3, /device:TPU:0, one launch (start us, length us, event | category | flops | bytes accessed | tf_op | source)
XLA Modules:
  0.0 38.9 jit_solution(4892356096799534890)
XLA Ops:
  0.0 7.2 %multiply_convert_fusion = bf16[16,64,8192]{2,1,0:T(8,128)(2,1)} fusion(f32[64,8192]{1,0:T(8,128)} %constant.9, f32[16,8192]{1,0:T(8,128)} %param.4), kind=kLoop, calls=%fused_computation | loop fusion | flops 16777216 | bytes 19398656 | tf_op jit(solution)/shard_map/while/body/eval_jaxpr/convert_element_type | solution.py:54
  7.2 14.4 %fusion.total = f32[1024,512]{1,0:T(8,128)S(1)} fusion(bf16[1024,8192]{1,0:T(8,128)(2,1)} %bitcast.4, bf16[512,8192]{1,0:T(8,128)(2,1)} %bitcast.5), kind=kOutput, calls=%fused_computation.1 | convolution fusion | flops 8589934592 | bytes 27262976 | tf_op jit(solution)/shard_map/while/body/eval_jaxpr/dot_general | solution.py:55
  21.7 0.9 %shift.2 = bf16[32,16,128]{2,1,0:T(8,128)(2,1)S(1)} custom-call(f32[1024,512]{1,0:T(8,128)S(1)} %fusion.total), custom_call_target="tpu_custom_call" | custom-call | tf_op jit(solution)/shard_map/while/body/eval_jaxpr/shift/pallas_call | solution.py:56
  22.6 15.3 %all_to_all.5.in_ref = bf16[32,16,128]{2,1,0:T(8,128)(2,1)S(1)} all-to-all(bf16[32,16,128]{2,1,0:T(8,128)(2,1)S(1)} %shift.2), channel_id=1, replica_groups=mesh['st'=8,'ta'=4] {'st','ta'}, dimensions={0} | all-to-all | bytes 262144 | tf_op jit(solution)/shard_map/all_to_all | solution.py:139
  37.9 1.0 %correlate.1 = bf16[1,2,128,128]{3,2,1,0:T(8,128)(2,1)} custom-call(bf16[32,16,128]{2,1,0:T(8,128)(2,1)S(1)} %all_to_all.5.in_ref), custom_call_target="tpu_custom_call" | custom-call | tf_op jit(solution)/shard_map/correlate/pallas_call | solution.py:123

commit v4 on v2

--- a/solution.py
+++ b/solution.py
@@ -23,7 +23,7 @@
     angles = 2.0 * math.pi / frame_len * phases
     parts = np.stack([np.cos(angles), -np.sin(angles)]) * frame_len**-0.5
     blocks = parts.reshape(2, channel_count // CHANNEL_BLOCK, CHANNEL_BLOCK, frame_len)
-    return blocks.transpose(1, 0, 2, 3).reshape(-1, 2 * CHANNEL_BLOCK, frame_len).astype(np.float32)
+    return blocks.transpose(1, 0, 2, 3).reshape(-1, 2 * CHANNEL_BLOCK, frame_len).astype(jnp.bfloat16)
 
 
 def channelize_kernel(frame_count, x_ref, coef_ref, table_ref, out_ref, folded, total, turned):
@@ -32,7 +32,7 @@
     rows = table_ref.shape[1]
     table = table_ref[0]
     for tap in range(taps):
-        folded[tap * rows : (tap + 1) * rows, :] = (table * coef_ref[tap : tap + 1, :]).astype(jnp.bfloat16)
+        folded[tap * rows : (tap + 1) * rows, :] = table * coef_ref[tap : tap + 1, :].astype(jnp.bfloat16)
     product = lax.dot_general(folded[...], x_ref[...], NT, preferred_element_type=jnp.float32)
 
     @pl.when(step == 0)
@@ -156,7 +156,7 @@
         out_specs=pl.BlockSpec(memory_space=pltpu.VMEM),
         out_shape=jax.ShapeDtypeStruct((1, 2, all_inputs, all_inputs), jnp.bfloat16),
         scratch_shapes=[pltpu.VMEM((2 * all_inputs, ta_count * frame_count), jnp.float32)],
-        compiler_params=pltpu.CompilerParams(vmem_limit_bytes=VMEM_LIMIT),
+        compiler_params=pltpu.CompilerParams(vmem_limit_bytes=32 * 1024 * 1024),
         name="correlate",
     )(arrived)
 

time: 31.2 us -> 30.1 us (0.965)
  Pallas kernels: 15.4 us -> 14.4 us
    pallas_call x1, Pallas kernels: 1.87 us -> 0.97 us  [correlate(): pl.pallas_call(functools.partial(correlate_kernel, frame_count, st_count,...]
where the time goes in v4:
time: 30.1 us; the launch traced here: 29.9 us
  blocking collectives  15.5 us (51%)
  Pallas kernels  14.4 us (48%)
    all_to_all x1, blocking collectives, on_device(): lax.all_to_all(partial, ('st', 'ta'), split_axis=0, concat_axis=0, tiled=...  15.5 us
    pallas_call x1, Pallas kernels, channelize(): pl.pallas_call(functools.partial(channelize_kernel, frame_count), grid=(b...  13.4 us
    pallas_call x1, Pallas kernels, correlate(): pl.pallas_call(functools.partial(correlate_kernel, frame_count, st_count,...  0.97 us

profile of v4, /device:TPU:0, one launch (start us, length us, event | category | flops | bytes accessed | tf_op | source)
XLA Modules:
  0.0 29.9 jit_solution(8336531578159924349)
XLA Ops:
  0.0 13.4 %channelize.1 = bf16[32,16,128]{2,1,0:T(8,128)(2,1)} custom-call(bf16[512,8192]{1,0:T(8,128)(2,1)} %bitcast.1, f32[16,8192]{1,0:T(8,128)} %coef_ref.1, bf16[1,64,8192]{2,1,0:T(8,128)(2,1)} %constant.2.clone.table_ref), custom_call_target="tpu_custom_call" | custom-call | flops 8589934592 | bytes 8388608 | tf_op jit(solution)/shard_map/channelize/pallas_call | solution.py:78
  13.4 15.5 %all_to_all.5.in_ref = bf16[32,16,128]{2,1,0:T(8,128)(2,1)S(1)} all-to-all(bf16[32,16,128]{2,1,0:T(8,128)(2,1)} %channelize.1), channel_id=1, replica_groups=mesh['st'=8,'ta'=4] {'st','ta'}, dimensions={0} | all-to-all | bytes 262144 | tf_op jit(solution)/shard_map/all_to_all | solution.py:169
  29.0 1.0 %correlate.1 = bf16[1,2,128,128]{3,2,1,0:T(8,128)(2,1)} custom-call(bf16[32,16,128]{2,1,0:T(8,128)(2,1)S(1)} %all_to_all.5.in_ref), custom_call_target="tpu_custom_call" | custom-call | tf_op jit(solution)/shard_map/correlate/pallas_call | solution.py:153

commit v5 on v2

--- a/solution.py
+++ b/solution.py
@@ -13,6 +13,7 @@
 LANES = 128
 CHANNEL_BLOCK = 32
 K_BLOCK = 2048
+TILE = 256
 VMEM_LIMIT = 60 * 1024 * 1024
 NT = (((1,), (1,)), ((), ()))
 
@@ -33,15 +34,17 @@
     table = table_ref[0]
     for tap in range(taps):
         folded[tap * rows : (tap + 1) * rows, :] = (table * coef_ref[tap : tap + 1, :]).astype(jnp.bfloat16)
-    product = lax.dot_general(folded[...], x_ref[...], NT, preferred_element_type=jnp.float32)
 
     @pl.when(step == 0)
     def _():
-        total[...] = product
+        total[...] = jnp.zeros_like(total)
 
-    @pl.when(step > 0)
-    def _():
-        total[...] += product
+    for first in range(0, taps * rows, TILE):
+        for column in range(0, total.shape[1], TILE):
+            product = lax.dot_general(
+                folded[first : first + TILE, :], x_ref[column : column + TILE, :], NT, preferred_element_type=jnp.float32
+            )
+            total[first : first + TILE, column : column + TILE] += product
 
     @pl.when(step == pl.num_programs(1) - 1)
     def _():
@@ -156,7 +159,7 @@
         out_specs=pl.BlockSpec(memory_space=pltpu.VMEM),
         out_shape=jax.ShapeDtypeStruct((1, 2, all_inputs, all_inputs), jnp.bfloat16),
         scratch_shapes=[pltpu.VMEM((2 * all_inputs, ta_count * frame_count), jnp.float32)],
-        compiler_params=pltpu.CompilerParams(vmem_limit_bytes=VMEM_LIMIT),
+        compiler_params=pltpu.CompilerParams(vmem_limit_bytes=32 * 1024 * 1024),
         name="correlate",
     )(arrived)
 

time: 31.2 us -> 32 us (1.026)
  Pallas kernels: 15.4 us -> 16.3 us
    pallas_call x1, Pallas kernels: 13.5 us -> 15.3 us  [channelize(): pl.pallas_call(functools.partial(channelize_kernel, frame_count), grid=(b...]
    pallas_call x1, Pallas kernels: 1.87 us -> 0.97 us  [correlate(): pl.pallas_call(functools.partial(correlate_kernel, frame_count, st_count,...]
where the time goes in v5:
time: 32 us; the launch traced here: 31.9 us
  Pallas kernels  16.3 us (51%)
  blocking collectives  15.5 us (48%)
    all_to_all x1, blocking collectives, on_device(): lax.all_to_all(partial, ('st', 'ta'), split_axis=0, concat_axis=0, tiled=...  15.5 us
    pallas_call x1, Pallas kernels, channelize(): pl.pallas_call(functools.partial(channelize_kernel, frame_count), grid=(b...  15.3 us
    pallas_call x1, Pallas kernels, correlate(): pl.pallas_call(functools.partial(correlate_kernel, frame_count, st_count,...  0.97 us

profile of v5, /device:TPU:0, one launch (start us, length us, event | category | flops | bytes accessed | tf_op | source)
XLA Modules:
  0.0 31.9 jit_solution(5319979016005432332)
XLA Ops:
  0.0 15.3 %channelize.1 = bf16[32,16,128]{2,1,0:T(8,128)(2,1)} custom-call(bf16[512,8192]{1,0:T(8,128)(2,1)} %bitcast.1, f32[16,8192]{1,0:T(8,128)} %coef_ref.1, f32[1,64,8192]{2,1,0:T(8,128)} %constant.2.clone.table_ref), custom_call_target="tpu_custom_call" | custom-call | flops 8589934592 | bytes 8388608 | tf_op jit(solution)/shard_map/channelize/pallas_call | solution.py:81
  15.3 15.5 %all_to_all.5.in_ref = bf16[32,16,128]{2,1,0:T(8,128)(2,1)S(1)} all-to-all(bf16[32,16,128]{2,1,0:T(8,128)(2,1)} %channelize.1), channel_id=1, replica_groups=mesh['st'=8,'ta'=4] {'st','ta'}, dimensions={0} | all-to-all | bytes 262144 | tf_op jit(solution)/shard_map/all_to_all | solution.py:172
  30.9 1.0 %correlate.1 = bf16[1,2,128,128]{3,2,1,0:T(8,128)(2,1)} custom-call(bf16[32,16,128]{2,1,0:T(8,128)(2,1)S(1)} %all_to_all.5.in_ref), custom_call_target="tpu_custom_call" | custom-call | tf_op jit(solution)/shard_map/correlate/pallas_call | solution.py:156

commit v6 on v5

v6 whole, which is shorter than its diff:
```python
import functools
import math

import jax
import jax.numpy as jnp
import numpy as np
from jax import lax
from jax.experimental import pallas as pl
from jax.experimental.pallas import tpu as pltpu
from jax.sharding import PartitionSpec as P

CH0 = 1024
LANES = 128
CHANNEL_BLOCK = 32
K_BLOCK = 2048
VMEM_LIMIT = 60 * 1024 * 1024
NT = (((1,), (1,)), ((), ()))


def phase_table(frame_len, channel_count, first_channel):
    channels = first_channel + np.arange(channel_count, dtype=np.int64)
    phases = (channels[:, None] * np.arange(frame_len, dtype=np.int64)[None, :]) % frame_len
    angles = 2.0 * math.pi / frame_len * phases
    parts = np.stack([np.cos(angles), -np.sin(angles)]) * frame_len**-0.5
    blocks = parts.reshape(2, channel_count // CHANNEL_BLOCK, CHANNEL_BLOCK, frame_len)
    return blocks.transpose(1, 0, 2, 3).reshape(-1, 2 * CHANNEL_BLOCK, frame_len).astype(np.float32)


def channelize_kernel(frame_count, x_ref, coef_ref, table_ref, out_ref, halves, folded, total, turned):
    step = pl.program_id(1)
    taps = coef_ref.shape[0]
    half = taps // 2
    rows = table_ref.shape[1]
    pairs = frame_count // taps
    inputs = x_ref.shape[0] // frame_count

    for pair in range(pairs):
        for first in range(0, inputs, 2):
            blocks = []
            for place in (first, first + 1):
                row = place * frame_count + pair * taps
                blocks.append(x_ref[row : row + taps, :].astype(jnp.float32))
            even = jnp.concatenate([block[:half] for block in blocks], 0)
            odd = jnp.concatenate([block[half:] for block in blocks], 0)
            row = (pair * inputs + first) * half
            for kind, value in enumerate((even, odd, even + odd)):
                halves[kind, row : row + taps, :] = value.astype(jnp.bfloat16)

    table = table_ref[0]
    for tap in range(half):
        low = coef_ref[tap : tap + 1, :]
        high = coef_ref[half + tap : half + tap + 1, :]
        for kind, coef in enumerate((high, low, low + high)):
            folded[kind, tap * rows : (tap + 1) * rows, :] = (table * coef).astype(jnp.bfloat16)

    @pl.when(step == 0)
    def _():
        total[...] = jnp.zeros_like(total)

    for kind in range(3):
        total[kind] += lax.dot_general(folded[kind], halves[kind], NT, preferred_element_type=jnp.float32)

    @pl.when(step == pl.num_programs(1) - 1)
    def _():
        frame = lax.broadcasted_iota(jnp.int32, (rows, LANES), 1) % half

        def shifted_sum(kind, pair):
            lanes = slice(pair * LANES, (pair + 1) * LANES)
            both = total[kind, 0:rows, lanes]
            inside = both
            for tap in range(1, half):
                moved = pltpu.roll(total[kind, tap * rows : (tap + 1) * rows, lanes], LANES - tap, 1)
                both = both + moved
                inside = inside + jnp.where(frame < half - tap, moved, 0.0)
            return inside, both - inside

        inside = {}
        before = {}
        for pair in range(pairs):
            (p0, c0), (p1, c1), (p2, c2) = (shifted_sum(kind, pair) for kind in range(3))
            for place, now, carry in (
                (2 * pair - 1, p0, c0),
                (2 * pair, p2 - p0 - p1, c2 - c0 - c1),
                (2 * pair + 1, p1, c1),
            ):
                inside[place] = inside[place] + now if place in inside else now
                before[place - 1] = before[place - 1] + carry if place - 1 in before else carry
        count = 2 * pairs
        channels = rows // 2
        slots = 4 * count
        for place in range(-2, count):
            value = inside.get(place)
            if place in before:
                carry = pltpu.roll(before[place], half, 1)
                value = carry if value is None else value + carry
            for part in range(2):
                slot = part * count + place if place >= 0 else (3 + part) * count + place
                turned[pl.ds(slot, channels, stride=slots), :] = value[part * channels : (part + 1) * channels]
        nothing = jnp.zeros((channels, LANES), jnp.float32)
        for part in range(2):
            for place in range(count - 2):
                turned[pl.ds((2 + part) * count + place, channels, stride=slots), :] = nothing
        out_ref[...] = turned[...].astype(jnp.bfloat16).reshape(out_ref.shape)


def channelize(samples, coefficients, channel_count):
    inputs, frame_count, frame_len = samples.shape
    taps = coefficients.shape[0]
    half = taps // 2
    rows = 2 * CHANNEL_BLOCK
    columns = inputs * frame_count
    blocks = channel_count // CHANNEL_BLOCK
    slots = 4 * frame_count // half
    k_block = min(K_BLOCK, frame_len)
    assert inputs * half == LANES and frame_count % taps == 0
    table = jnp.asarray(phase_table(frame_len, channel_count, CH0))
    return pl.pallas_call(
        functools.partial(channelize_kernel, frame_count),
        grid=(blocks, frame_len // k_block),
        in_specs=[
            pl.BlockSpec((columns, k_block), lambda b, k: (0, k)),
            pl.BlockSpec((taps, k_block), lambda b, k: (0, k)),
            pl.BlockSpec((1, rows, k_block), lambda b, k: (b, 0, k)),
        ],
        out_specs=pl.BlockSpec((CHANNEL_BLOCK, slots, LANES), lambda b, k: (b, 0, 0)),
        out_shape=jax.ShapeDtypeStruct((channel_count, slots, LANES), jnp.bfloat16),
        scratch_shapes=[
            pltpu.VMEM((3, columns // 2, k_block), jnp.bfloat16),
            pltpu.VMEM((3, half * rows, k_block), jnp.bfloat16),
            pltpu.VMEM((3, half * rows, columns // 2), jnp.float32),
            pltpu.VMEM((CHANNEL_BLOCK * slots, LANES), jnp.float32),
        ],
        compiler_params=pltpu.CompilerParams(
            dimension_semantics=("arbitrary", "arbitrary"), vmem_limit_bytes=VMEM_LIMIT
        ),
        cost_estimate=pl.CostEstimate(
            flops=3 * channel_count * taps * columns * frame_len,
            bytes_accessed=2 * columns * frame_len,
            transcendentals=0,
        ),
        name="channelize",
    )(samples.reshape(columns, frame_len), coefficients, table)


def correlate_kernel(half, st_count, ta_count, in_ref, out_ref, arranged, across, spectra):
    slots = in_ref.shape[1] // 2
    count = slots // 2
    inputs = LANES // half
    places = ta_count * count
    stations = LANES // places
    all_inputs = st_count * inputs
    position = lax.broadcasted_iota(jnp.int32, (inputs, LANES), 1) // places

    def station_group(group):
        for place in range(stations):
            st = group * stations + place
            for ta in range(ta_count):
                value = in_ref[st * ta_count + ta].astype(jnp.float32)[:slots]
                if ta < ta_count - 1:
                    value = value + in_ref[st * ta_count + ta + 1].astype(jnp.float32)[slots:]
                for part in range(2):
                    row = place * places + ta * count
                    arranged[part, row : row + count, :] = value[part * count : (part + 1) * count]
        for part in range(2):
            across[part] = arranged[part].T
            by_frame = [across[part, pl.ds(frame, inputs, stride=half), :] for frame in range(half)]
            for place in range(stations):
                result = None
                for frame in range(half):
                    shift = ((frame - place) * places) % LANES
                    value = pltpu.roll(by_frame[frame], shift, 1) if shift else by_frame[frame]
                    result = value if result is None else jnp.where(position == frame, value, result)
                first = part * all_inputs + (group * stations + place) * inputs
                if not isinstance(first, int):
                    first = pl.multiple_of(first, inputs)
                spectra[pl.ds(first, inputs), :] = result

    if st_count == stations:
        station_group(0)
    else:
        lax.fori_loop(0, st_count // stations, lambda group, _: (station_group(group), 0)[1], 0)
    real_part = spectra[:all_inputs, :].astype(jnp.bfloat16)
    imag_part = spectra[all_inputs:, :].astype(jnp.bfloat16)
    right = jnp.concatenate([real_part, imag_part], 1)
    left = jnp.concatenate([imag_part, -real_part], 1)
    scale = 1.0 / LANES
    for part, rows in enumerate((right, left)):
        product = lax.dot_general(rows, right, NT, preferred_element_type=jnp.float32)
        out_ref[0, part] = (product * scale).astype(jnp.bfloat16)


def correlate(arrived, half, frame_count, st_count, ta_count, all_inputs):
    assert ta_count * frame_count == LANES
    return pl.pallas_call(
        functools.partial(correlate_kernel, half, st_count, ta_count),
        in_specs=[pl.BlockSpec(memory_space=pltpu.VMEM)],
        out_specs=pl.BlockSpec(memory_space=pltpu.VMEM),
        out_shape=jax.ShapeDtypeStruct((1, 2, all_inputs, all_inputs), jnp.bfloat16),
        scratch_shapes=[
            pltpu.VMEM((2, LANES, LANES), jnp.float32),
            pltpu.VMEM((2, LANES, LANES), jnp.float32),
            pltpu.VMEM((2 * all_inputs, LANES), jnp.float32),
        ],
        compiler_params=pltpu.CompilerParams(vmem_limit_bytes=32 * 1024 * 1024),
        name="correlate",
    )(arrived)


def on_device(samples, coefficients):
    st_count = lax.axis_size("st")
    ta_count = lax.axis_size("ta")
    inputs, frame_count, _ = samples.shape
    partial = channelize(samples, coefficients, st_count * ta_count)
    arrived = lax.all_to_all(partial, ("st", "ta"), split_axis=0, concat_axis=0, tiled=True)
    return correlate(arrived, coefficients.shape[0] // 2, frame_count, st_count, ta_count, st_count * inputs)


def solution(mesh):
    return jax.shard_map(
        on_device,
        mesh=mesh,
        in_specs=(P("st", "ta", None), P()),
        out_specs=P(("st", "ta"), None, None, None),
        check_vma=False,
    )
```

time: 32 us -> 32 us (level)
  no operation moved by 1% of the time
where the time goes in v6:
time: 32 us; the launch traced here: 31.9 us
  Pallas kernels  16.3 us (51%)
  blocking collectives  15.5 us (48%)
    all_to_all x1, blocking collectives, on_device(): lax.all_to_all(partial, ('st', 'ta'), split_axis=0, concat_axis=0, tiled=...  15.5 us
    pallas_call x1, Pallas kernels, channelize(): pl.pallas_call(functools.partial(channelize_kernel, frame_count), grid=(b...  15.2 us
    pallas_call x1, Pallas kernels, correlate(): pl.pallas_call(functools.partial(correlate_kernel, half, st_count, ta_cou...  1.11 us

profile of v6, /device:TPU:0, one launch (start us, length us, event | category | flops | bytes accessed | tf_op | source)
XLA Modules:
  0.0 31.9 jit_solution(5283916613749333642)
XLA Ops:
  0.0 15.2 %channelize.1 = bf16[32,16,128]{2,1,0:T(8,128)(2,1)} custom-call(bf16[512,8192]{1,0:T(8,128)(2,1)} %bitcast.1, f32[16,8192]{1,0:T(8,128)} %coef_ref.1, f32[1,64,8192]{2,1,0:T(8,128)} %constant.2.clone.table_ref), custom_call_target="tpu_custom_call" | custom-call | flops 6442450944 | bytes 8388608 | tf_op jit(solution)/shard_map/channelize/pallas_call | solution.py:117
  15.2 15.5 %all_to_all.5.in_ref = bf16[32,16,128]{2,1,0:T(8,128)(2,1)S(1)} all-to-all(bf16[32,16,128]{2,1,0:T(8,128)(2,1)} %channelize.1), channel_id=1, replica_groups=mesh['st'=8,'ta'=4] {'st','ta'}, dimensions={0} | all-to-all | bytes 262144 | tf_op jit(solution)/shard_map/all_to_all | solution.py:214
  30.7 1.1 %correlate.1 = bf16[1,2,128,128]{3,2,1,0:T(8,128)(2,1)} custom-call(bf16[32,16,128]{2,1,0:T(8,128)(2,1)S(1)} %all_to_all.5.in_ref), custom_call_target="tpu_custom_call" | custom-call | tf_op jit(solution)/shard_map/correlate/pallas_call | solution.py:194

commit v7 on v5

--- a/solution.py
+++ b/solution.py
@@ -13,7 +13,6 @@
 LANES = 128
 CHANNEL_BLOCK = 32
 K_BLOCK = 2048
-TILE = 256
 VMEM_LIMIT = 60 * 1024 * 1024
 NT = (((1,), (1,)), ((), ()))
 
@@ -27,24 +26,20 @@
     return blocks.transpose(1, 0, 2, 3).reshape(-1, 2 * CHANNEL_BLOCK, frame_len).astype(np.float32)
 
 
-def channelize_kernel(frame_count, x_ref, coef_ref, table_ref, out_ref, folded, total, turned):
+def channelize_kernel(frame_count, x_ref, coef_ref, table_ref, out_ref, total, turned):
     step = pl.program_id(1)
     taps = coef_ref.shape[0]
     rows = table_ref.shape[1]
     table = table_ref[0]
-    for tap in range(taps):
-        folded[tap * rows : (tap + 1) * rows, :] = (table * coef_ref[tap : tap + 1, :]).astype(jnp.bfloat16)
+    folded = jnp.concatenate(
+        [(table * coef_ref[tap : tap + 1, :]).astype(jnp.bfloat16) for tap in range(taps)], 0
+    )
 
     @pl.when(step == 0)
     def _():
         total[...] = jnp.zeros_like(total)
 
-    for first in range(0, taps * rows, TILE):
-        for column in range(0, total.shape[1], TILE):
-            product = lax.dot_general(
-                folded[first : first + TILE, :], x_ref[column : column + TILE, :], NT, preferred_element_type=jnp.float32
-            )
-            total[first : first + TILE, column : column + TILE] += product
+    total[...] += lax.dot_general(folded, x_ref[...], NT, preferred_element_type=jnp.float32)
 
     @pl.when(step == pl.num_programs(1) - 1)
     def _():
@@ -89,7 +84,6 @@
         out_specs=pl.BlockSpec((CHANNEL_BLOCK, slots, LANES), lambda b, k: (b, 0, 0)),
         out_shape=jax.ShapeDtypeStruct((channel_count, slots, LANES), jnp.bfloat16),
         scratch_shapes=[
-            pltpu.VMEM((taps * rows, k_block), jnp.bfloat16),
             pltpu.VMEM((taps * rows, columns), jnp.float32),
             pltpu.VMEM((CHANNEL_BLOCK * slots, LANES), jnp.float32),
         ],

time: 32 us -> 33.7 us (1.053)
  Pallas kernels: 16.3 us -> 18 us
    pallas_call x1, Pallas kernels: 15.3 us -> 17 us  [channelize(): pl.pallas_call(functools.partial(channelize_kernel, frame_count), grid=(b...]
where the time goes in v7:
time: 33.7 us; the launch traced here: 33.5 us
  Pallas kernels  18 us (53%)
  blocking collectives  15.5 us (46%)
    pallas_call x1, Pallas kernels, channelize(): pl.pallas_call(functools.partial(channelize_kernel, frame_count), grid=(b...  17 us
    all_to_all x1, blocking collectives, on_device(): lax.all_to_all(partial, ('st', 'ta'), split_axis=0, concat_axis=0, tiled=...  15.5 us
    pallas_call x1, Pallas kernels, correlate(): pl.pallas_call(functools.partial(correlate_kernel, frame_count, st_count,...  0.97 us

profile of v7, /device:TPU:0, one launch (start us, length us, event | category | flops | bytes accessed | tf_op | source)
XLA Modules:
  0.0 33.5 jit_solution(4457823228144965133)
XLA Ops:
  0.0 17.0 %channelize.1 = bf16[32,16,128]{2,1,0:T(8,128)(2,1)} custom-call(bf16[512,8192]{1,0:T(8,128)(2,1)} %bitcast.1, f32[16,8192]{1,0:T(8,128)} %coef_ref.1, f32[1,64,8192]{2,1,0:T(8,128)} %constant.2.clone.table_ref), custom_call_target="tpu_custom_call" | custom-call | flops 8589934592 | bytes 8388608 | tf_op jit(solution)/shard_map/channelize/pallas_call | solution.py:76
  17.0 15.5 %all_to_all.5.in_ref = bf16[32,16,128]{2,1,0:T(8,128)(2,1)S(1)} all-to-all(bf16[32,16,128]{2,1,0:T(8,128)(2,1)} %channelize.1), channel_id=1, replica_groups=mesh['st'=8,'ta'=4] {'st','ta'}, dimensions={0} | all-to-all | bytes 262144 | tf_op jit(solution)/shard_map/all_to_all | solution.py:166
  32.5 1.0 %correlate.1 = bf16[1,2,128,128]{3,2,1,0:T(8,128)(2,1)} custom-call(bf16[32,16,128]{2,1,0:T(8,128)(2,1)S(1)} %all_to_all.5.in_ref), custom_call_target="tpu_custom_call" | custom-call | tf_op jit(solution)/shard_map/correlate/pallas_call | solution.py:150

commit v8 on v6

--- a/solution.py
+++ b/solution.py
@@ -53,12 +53,19 @@
         for kind, coef in enumerate((high, low, low + high)):
             folded[kind, tap * rows : (tap + 1) * rows, :] = (table * coef).astype(jnp.bfloat16)
 
+    products = [
+        lax.dot_general(folded[kind], halves[kind], NT, preferred_element_type=jnp.float32) for kind in range(3)
+    ]
+
     @pl.when(step == 0)
     def _():
-        total[...] = jnp.zeros_like(total)
-
-    for kind in range(3):
-        total[kind] += lax.dot_general(folded[kind], halves[kind], NT, preferred_element_type=jnp.float32)
+        for kind in range(3):
+            total[kind] = products[kind]
+
+    @pl.when(step > 0)
+    def _():
+        for kind in range(3):
+            total[kind] += products[kind]
 
     @pl.when(step == pl.num_programs(1) - 1)
     def _():

time: 32 us -> 27.7 us (0.87)
  Pallas kernels: 16.3 us -> 12 us
    pallas_call x1, Pallas kernels: 15.2 us -> 10.9 us  [channelize(): pl.pallas_call(functools.partial(channelize_kernel, frame_count), grid=(b...]
where the time goes in v8:
time: 27.7 us; the launch traced here: 27.5 us
  blocking collectives  15.5 us (56%)
  Pallas kernels  12 us (43%)
    all_to_all x1, blocking collectives, on_device(): lax.all_to_all(partial, ('st', 'ta'), split_axis=0, concat_axis=0, tiled=...  15.5 us
    pallas_call x1, Pallas kernels, channelize(): pl.pallas_call(functools.partial(channelize_kernel, frame_count), grid=(b...  10.9 us
    pallas_call x1, Pallas kernels, correlate(): pl.pallas_call(functools.partial(correlate_kernel, half, st_count, ta_cou...  1.11 us

profile of v8, /device:TPU:0, one launch (start us, length us, event | category | flops | bytes accessed | tf_op | source)
XLA Modules:
  0.0 27.5 jit_solution(15743908828034454508)
XLA Ops:
  0.0 10.9 %channelize.1 = bf16[32,16,128]{2,1,0:T(8,128)(2,1)} custom-call(bf16[512,8192]{1,0:T(8,128)(2,1)} %bitcast.1, f32[16,8192]{1,0:T(8,128)} %coef_ref.1, f32[1,64,8192]{2,1,0:T(8,128)} %constant.2.clone.table_ref), custom_call_target="tpu_custom_call" | custom-call | flops 6442450944 | bytes 8388608 | tf_op jit(solution)/shard_map/channelize/pallas_call | solution.py:124
  10.9 15.5 %all_to_all.5.in_ref = bf16[32,16,128]{2,1,0:T(8,128)(2,1)S(1)} all-to-all(bf16[32,16,128]{2,1,0:T(8,128)(2,1)} %channelize.1), channel_id=1, replica_groups=mesh['st'=8,'ta'=4] {'st','ta'}, dimensions={0} | all-to-all | bytes 262144 | tf_op jit(solution)/shard_map/all_to_all | solution.py:221
  26.4 1.1 %correlate.1 = bf16[1,2,128,128]{3,2,1,0:T(8,128)(2,1)} custom-call(bf16[32,16,128]{2,1,0:T(8,128)(2,1)S(1)} %all_to_all.5.in_ref), custom_call_target="tpu_custom_call" | custom-call | tf_op jit(solution)/shard_map/correlate/pallas_call | solution.py:201

commit v9 on v6

--- a/solution.py
+++ b/solution.py
@@ -53,12 +53,10 @@
         for kind, coef in enumerate((high, low, low + high)):
             folded[kind, tap * rows : (tap + 1) * rows, :] = (table * coef).astype(jnp.bfloat16)
 
-    @pl.when(step == 0)
-    def _():
-        total[...] = jnp.zeros_like(total)
-
     for kind in range(3):
-        total[kind] += lax.dot_general(folded[kind], halves[kind], NT, preferred_element_type=jnp.float32)
+        total[step, kind] = lax.dot_general(
+            folded[kind], halves[kind], NT, preferred_element_type=jnp.float32
+        )
 
     @pl.when(step == pl.num_programs(1) - 1)
     def _():
@@ -66,10 +64,15 @@
 
         def shifted_sum(kind, pair):
             lanes = slice(pair * LANES, (pair + 1) * LANES)
-            both = total[kind, 0:rows, lanes]
+
+            def summed(tap):
+                slots = [total[chunk, kind, tap * rows : (tap + 1) * rows, lanes] for chunk in range(total.shape[0])]
+                return functools.reduce(jnp.add, slots)
+
+            both = summed(0)
             inside = both
             for tap in range(1, half):
-                moved = pltpu.roll(total[kind, tap * rows : (tap + 1) * rows, lanes], LANES - tap, 1)
+                moved = pltpu.roll(summed(tap), LANES - tap, 1)
                 both = both + moved
                 inside = inside + jnp.where(frame < half - tap, moved, 0.0)
             return inside, both - inside
@@ -127,7 +130,7 @@
         scratch_shapes=[
             pltpu.VMEM((3, columns // 2, k_block), jnp.bfloat16),
             pltpu.VMEM((3, half * rows, k_block), jnp.bfloat16),
-            pltpu.VMEM((3, half * rows, columns // 2), jnp.float32),
+            pltpu.VMEM((frame_len // k_block, 3, half * rows, columns // 2), jnp.float32),
             pltpu.VMEM((CHANNEL_BLOCK * slots, LANES), jnp.float32),
         ],
         compiler_params=pltpu.CompilerParams(

time: 32 us -> 27.2 us (0.85)
  Pallas kernels: 16.3 us -> 11.5 us
    pallas_call x1, Pallas kernels: 15.2 us -> 10.4 us  [channelize(): pl.pallas_call(functools.partial(channelize_kernel, frame_count), grid=(b...]
where the time goes in v9:
time: 27.2 us; the launch traced here: 27 us
  blocking collectives  15.5 us (57%)
  Pallas kernels  11.5 us (42%)
    all_to_all x1, blocking collectives, on_device(): lax.all_to_all(partial, ('st', 'ta'), split_axis=0, concat_axis=0, tiled=...  15.5 us
    pallas_call x1, Pallas kernels, channelize(): pl.pallas_call(functools.partial(channelize_kernel, frame_count), grid=(b...  10.4 us
    pallas_call x1, Pallas kernels, correlate(): pl.pallas_call(functools.partial(correlate_kernel, half, st_count, ta_cou...  1.11 us

profile of v9, /device:TPU:0, one launch (start us, length us, event | category | flops | bytes accessed | tf_op | source)
XLA Modules:
  0.0 27.0 jit_solution(13727514376848432131)
XLA Ops:
  0.0 10.4 %channelize.1 = bf16[32,16,128]{2,1,0:T(8,128)(2,1)} custom-call(bf16[512,8192]{1,0:T(8,128)(2,1)} %bitcast.1, f32[16,8192]{1,0:T(8,128)} %coef_ref.1, f32[1,64,8192]{2,1,0:T(8,128)} %constant.2.clone.table_ref), custom_call_target="tpu_custom_call" | custom-call | flops 6442450944 | bytes 8388608 | tf_op jit(solution)/shard_map/channelize/pallas_call | solution.py:120
  10.4 15.5 %all_to_all.5.in_ref = bf16[32,16,128]{2,1,0:T(8,128)(2,1)S(1)} all-to-all(bf16[32,16,128]{2,1,0:T(8,128)(2,1)} %channelize.1), channel_id=1, replica_groups=mesh['st'=8,'ta'=4] {'st','ta'}, dimensions={0} | all-to-all | bytes 262144 | tf_op jit(solution)/shard_map/all_to_all | solution.py:217
  25.9 1.1 %correlate.1 = bf16[1,2,128,128]{3,2,1,0:T(8,128)(2,1)} custom-call(bf16[32,16,128]{2,1,0:T(8,128)(2,1)S(1)} %all_to_all.5.in_ref), custom_call_target="tpu_custom_call" | custom-call | tf_op jit(solution)/shard_map/correlate/pallas_call | solution.py:197

commit v10 on v9

--- a/solution.py
+++ b/solution.py
@@ -34,29 +34,24 @@
     pairs = frame_count // taps
     inputs = x_ref.shape[0] // frame_count
 
-    for pair in range(pairs):
-        for first in range(0, inputs, 2):
-            blocks = []
-            for place in (first, first + 1):
-                row = place * frame_count + pair * taps
-                blocks.append(x_ref[row : row + taps, :].astype(jnp.float32))
-            even = jnp.concatenate([block[:half] for block in blocks], 0)
-            odd = jnp.concatenate([block[half:] for block in blocks], 0)
-            row = (pair * inputs + first) * half
-            for kind, value in enumerate((even, odd, even + odd)):
-                halves[kind, row : row + taps, :] = value.astype(jnp.bfloat16)
-
     table = table_ref[0]
-    for tap in range(half):
-        low = coef_ref[tap : tap + 1, :]
-        high = coef_ref[half + tap : half + tap + 1, :]
-        for kind, coef in enumerate((high, low, low + high)):
+    for kind in range(3):
+        for pair in range(pairs):
+            for first in range(0, inputs, 2):
+                blocks = []
+                for place in (first, first + 1):
+                    row = place * frame_count + pair * taps
+                    blocks.append(x_ref[row : row + taps, :].astype(jnp.float32))
+                even = jnp.concatenate([block[:half] for block in blocks], 0)
+                odd = jnp.concatenate([block[half:] for block in blocks], 0)
+                row = (pair * inputs + first) * half
+                halves[kind, row : row + taps, :] = (even, odd, even + odd)[kind].astype(jnp.bfloat16)
+        for tap in range(half):
+            low = coef_ref[tap : tap + 1, :]
+            high = coef_ref[half + tap : half + tap + 1, :]
+            coef = (high, low, low + high)[kind]
             folded[kind, tap * rows : (tap + 1) * rows, :] = (table * coef).astype(jnp.bfloat16)
-
-    for kind in range(3):
-        total[step, kind] = lax.dot_general(
-            folded[kind], halves[kind], NT, preferred_element_type=jnp.float32
-        )
+        total[step, kind] = lax.dot_general(folded[kind], halves[kind], NT, preferred_element_type=jnp.float32)
 
     @pl.when(step == pl.num_programs(1) - 1)
     def _():

time: 27.2 us -> 27.2 us (level)
  no operation moved by 1% of the time
where the time goes in v10:
time: 27.2 us; the launch traced here: 27 us
  blocking collectives  15.5 us (57%)
  Pallas kernels  11.5 us (42%)
    all_to_all x1, blocking collectives, on_device(): lax.all_to_all(partial, ('st', 'ta'), split_axis=0, concat_axis=0, tiled=...  15.5 us
    pallas_call x1, Pallas kernels, channelize(): pl.pallas_call(functools.partial(channelize_kernel, frame_count), grid=(b...  10.4 us
    pallas_call x1, Pallas kernels, correlate(): pl.pallas_call(functools.partial(correlate_kernel, half, st_count, ta_cou...  1.11 us

profile of v10, /device:TPU:0, one launch (start us, length us, event | category | flops | bytes accessed | tf_op | source)
XLA Modules:
  0.0 27.0 jit_solution(12634044064042103337)
XLA Ops:
  0.0 10.4 %channelize.1 = bf16[32,16,128]{2,1,0:T(8,128)(2,1)} custom-call(bf16[512,8192]{1,0:T(8,128)(2,1)} %bitcast.1, f32[16,8192]{1,0:T(8,128)} %coef_ref.1, f32[1,64,8192]{2,1,0:T(8,128)} %constant.2.clone.table_ref), custom_call_target="tpu_custom_call" | custom-call | flops 6442450944 | bytes 8388608 | tf_op jit(solution)/shard_map/channelize/pallas_call | solution.py:115
  10.4 15.5 %all_to_all.5.in_ref = bf16[32,16,128]{2,1,0:T(8,128)(2,1)S(1)} all-to-all(bf16[32,16,128]{2,1,0:T(8,128)(2,1)} %channelize.1), channel_id=1, replica_groups=mesh['st'=8,'ta'=4] {'st','ta'}, dimensions={0} | all-to-all | bytes 262144 | tf_op jit(solution)/shard_map/all_to_all | solution.py:212
  25.9 1.1 %correlate.1 = bf16[1,2,128,128]{3,2,1,0:T(8,128)(2,1)} custom-call(bf16[32,16,128]{2,1,0:T(8,128)(2,1)S(1)} %all_to_all.5.in_ref), custom_call_target="tpu_custom_call" | custom-call | tf_op jit(solution)/shard_map/correlate/pallas_call | solution.py:192

commit v11 on v10

--- a/solution.py
+++ b/solution.py
@@ -13,6 +13,7 @@
 LANES = 128
 CHANNEL_BLOCK = 32
 K_BLOCK = 2048
+ROW_BLOCK = 256
 VMEM_LIMIT = 60 * 1024 * 1024
 NT = (((1,), (1,)), ((), ()))
 
@@ -51,7 +52,11 @@
             high = coef_ref[half + tap : half + tap + 1, :]
             coef = (high, low, low + high)[kind]
             folded[kind, tap * rows : (tap + 1) * rows, :] = (table * coef).astype(jnp.bfloat16)
-        total[step, kind] = lax.dot_general(folded[kind], halves[kind], NT, preferred_element_type=jnp.float32)
+        for first in range(0, half * rows, ROW_BLOCK):
+            part = slice(first, first + ROW_BLOCK)
+            total[step, kind, part, :] = lax.dot_general(
+                folded[kind, part, :], halves[kind], NT, preferred_element_type=jnp.float32
+            )
 
     @pl.when(step == pl.num_programs(1) - 1)
     def _():

time: 27.2 us -> 27.2 us (level)
  no operation moved by 1% of the time
where the time goes in v11:
time: 27.2 us; the launch traced here: 27 us
  blocking collectives  15.6 us (57%)
  Pallas kernels  11.5 us (42%)
    all_to_all x1, blocking collectives, on_device(): lax.all_to_all(partial, ('st', 'ta'), split_axis=0, concat_axis=0, tiled=...  15.6 us
    pallas_call x1, Pallas kernels, channelize(): pl.pallas_call(functools.partial(channelize_kernel, frame_count), grid=(b...  10.4 us
    pallas_call x1, Pallas kernels, correlate(): pl.pallas_call(functools.partial(correlate_kernel, half, st_count, ta_cou...  1.11 us

profile of v11, /device:TPU:0, one launch (start us, length us, event | category | flops | bytes accessed | tf_op | source)
XLA Modules:
  0.0 27.0 jit_solution(4727421695715149634)
XLA Ops:
  0.0 10.4 %channelize.1 = bf16[32,16,128]{2,1,0:T(8,128)(2,1)} custom-call(bf16[512,8192]{1,0:T(8,128)(2,1)} %bitcast.1, f32[16,8192]{1,0:T(8,128)} %coef_ref.1, f32[1,64,8192]{2,1,0:T(8,128)} %constant.2.clone.table_ref), custom_call_target="tpu_custom_call" | custom-call | flops 6442450944 | bytes 8388608 | tf_op jit(solution)/shard_map/channelize/pallas_call | solution.py:120
  10.4 15.6 %all_to_all.5.in_ref = bf16[32,16,128]{2,1,0:T(8,128)(2,1)S(1)} all-to-all(bf16[32,16,128]{2,1,0:T(8,128)(2,1)} %channelize.1), channel_id=1, replica_groups=mesh['st'=8,'ta'=4] {'st','ta'}, dimensions={0} | all-to-all | bytes 262144 | tf_op jit(solution)/shard_map/all_to_all | solution.py:217
  25.9 1.1 %correlate.1 = bf16[1,2,128,128]{3,2,1,0:T(8,128)(2,1)} custom-call(bf16[32,16,128]{2,1,0:T(8,128)(2,1)S(1)} %all_to_all.5.in_ref), custom_call_target="tpu_custom_call" | custom-call | tf_op jit(solution)/shard_map/correlate/pallas_call | solution.py:197

commit v12 on v10

--- a/solution.py
+++ b/solution.py
@@ -12,7 +12,7 @@
 CH0 = 1024
 LANES = 128
 CHANNEL_BLOCK = 32
-K_BLOCK = 2048
+K_BLOCK = 1024
 VMEM_LIMIT = 60 * 1024 * 1024
 NT = (((1,), (1,)), ((), ()))
 

time: 27.2 us -> 29.2 us (1.074)
  Pallas kernels: 11.5 us -> 13.3 us
    pallas_call x1, Pallas kernels: 10.4 us -> 12.2 us  [channelize(): pl.pallas_call(functools.partial(channelize_kernel, frame_count), grid=(b...]
where the time goes in v12:
time: 29.2 us; the launch traced here: 28.8 us
  blocking collectives  15.5 us (53%)
  Pallas kernels  13.3 us (46%)
    all_to_all x1, blocking collectives, on_device(): lax.all_to_all(partial, ('st', 'ta'), split_axis=0, concat_axis=0, tiled=...  15.5 us
    pallas_call x1, Pallas kernels, channelize(): pl.pallas_call(functools.partial(channelize_kernel, frame_count), grid=(b...  12.2 us
    pallas_call x1, Pallas kernels, correlate(): pl.pallas_call(functools.partial(correlate_kernel, half, st_count, ta_cou...  1.11 us

profile of v12, /device:TPU:0, one launch (start us, length us, event | category | flops | bytes accessed | tf_op | source)
XLA Modules:
  0.0 28.8 jit_solution(9583698531775327531)
XLA Ops:
  0.0 12.2 %channelize.1 = bf16[32,16,128]{2,1,0:T(8,128)(2,1)} custom-call(bf16[512,8192]{1,0:T(8,128)(2,1)} %bitcast.1, f32[16,8192]{1,0:T(8,128)} %coef_ref.1, f32[1,64,8192]{2,1,0:T(8,128)} %constant.2.clone.table_ref), custom_call_target="tpu_custom_call" | custom-call | flops 6442450944 | bytes 8388608 | tf_op jit(solution)/shard_map/channelize/pallas_call | solution.py:115
  12.2 15.5 %all_to_all.5.in_ref = bf16[32,16,128]{2,1,0:T(8,128)(2,1)S(1)} all-to-all(bf16[32,16,128]{2,1,0:T(8,128)(2,1)} %channelize.1), channel_id=1, replica_groups=mesh['st'=8,'ta'=4] {'st','ta'}, dimensions={0} | all-to-all | bytes 262144 | tf_op jit(solution)/shard_map/all_to_all | solution.py:212
  27.7 1.1 %correlate.1 = bf16[1,2,128,128]{3,2,1,0:T(8,128)(2,1)} custom-call(bf16[32,16,128]{2,1,0:T(8,128)(2,1)S(1)} %all_to_all.5.in_ref), custom_call_target="tpu_custom_call" | custom-call | tf_op jit(solution)/shard_map/correlate/pallas_call | solution.py:192

commit v13 on v6

--- a/solution.py
+++ b/solution.py
@@ -12,7 +12,6 @@
 CH0 = 1024
 LANES = 128
 CHANNEL_BLOCK = 32
-K_BLOCK = 2048
 VMEM_LIMIT = 60 * 1024 * 1024
 NT = (((1,), (1,)), ((), ()))
 
@@ -26,81 +25,94 @@
     return blocks.transpose(1, 0, 2, 3).reshape(-1, 2 * CHANNEL_BLOCK, frame_len).astype(np.float32)
 
 
-def channelize_kernel(frame_count, x_ref, coef_ref, table_ref, out_ref, halves, folded, total, turned):
-    step = pl.program_id(1)
-    taps = coef_ref.shape[0]
+def channelize_kernel(frame_count, cuts, x_hbm, coef_hbm, table_hbm, out_ref, x_in, coef_in, table_in, halves, folded, total, turned, sems):
+    block = pl.program_id(0)
+    taps = coef_hbm.shape[0]
     half = taps // 2
-    rows = table_ref.shape[1]
+    rows = table_hbm.shape[1]
     pairs = frame_count // taps
-    inputs = x_ref.shape[0] // frame_count
-
+    inputs = x_hbm.shape[0] // frame_count
+    chunks = [slice(first, last) for first, last in zip(cuts[:-1], cuts[1:])]
+    copies = []
+    for chunk, lanes in enumerate(chunks):
+        copies.append(
+            [
+                pltpu.make_async_copy(coef_hbm.at[:, lanes], coef_in.at[:, lanes], sems.at[chunk, 0]),
+                pltpu.make_async_copy(table_hbm.at[block, :, lanes], table_in.at[:, lanes], sems.at[chunk, 1]),
+                pltpu.make_async_copy(x_hbm.at[:, lanes], x_in.at[:, lanes], sems.at[chunk, 2]),
+            ]
+        )
+        for copy in copies[-1]:
+            copy.start()
+
+    for chunk, columns in enumerate(chunks):
+        for copy in copies[chunk]:
+            copy.wait()
+        table = table_in[:, columns]
+        for kind in range(3):
+            for pair in range(pairs):
+                for first in range(0, inputs, 2):
+                    blocks = []
+                    for place in (first, first + 1):
+                        row = place * frame_count + pair * taps
+                        blocks.append(x_in[row : row + taps, columns].astype(jnp.float32))
+                    even = jnp.concatenate([block[:half] for block in blocks], 0)
+                    odd = jnp.concatenate([block[half:] for block in blocks], 0)
+                    row = (pair * inputs + first) * half
+                    halves[kind, row : row + taps, columns] = (even, odd, even + odd)[kind].astype(jnp.bfloat16)
+            for tap in range(half):
+                low = coef_in[tap : tap + 1, columns]
+                high = coef_in[half + tap : half + tap + 1, columns]
+                coef = (high, low, low + high)[kind]
+                folded[kind, tap * rows : (tap + 1) * rows, columns] = (table * coef).astype(jnp.bfloat16)
+            total[chunk, kind] = lax.dot_general(
+                folded[kind, :, columns], halves[kind, :, columns], NT, preferred_element_type=jnp.float32
+            )
+
+    frame = lax.broadcasted_iota(jnp.int32, (rows, LANES), 1) % half
+
+    def shifted_sum(kind, pair):
+        lanes = slice(pair * LANES, (pair + 1) * LANES)
+
+        def summed(tap):
+            slots = [total[chunk, kind, tap * rows : (tap + 1) * rows, lanes] for chunk in range(total.shape[0])]
+            return functools.reduce(jnp.add, slots)
+
+        both = summed(0)
+        inside = both
+        for tap in range(1, half):
+            moved = pltpu.roll(summed(tap), LANES - tap, 1)
+            both = both + moved
+            inside = inside + jnp.where(frame < half - tap, moved, 0.0)
+        return inside, both - inside
+
+    inside = {}
+    before = {}
     for pair in range(pairs):
-        for first in range(0, inputs, 2):
-            blocks = []
-            for place in (first, first + 1):
-                row = place * frame_count + pair * taps
-                blocks.append(x_ref[row : row + taps, :].astype(jnp.float32))
-            even = jnp.concatenate([block[:half] for block in blocks], 0)
-            odd = jnp.concatenate([block[half:] for block in blocks], 0)
-            row = (pair * inputs + first) * half
-            for kind, value in enumerate((even, odd, even + odd)):
-                halves[kind, row : row + taps, :] = value.astype(jnp.bfloat16)
-
-    table = table_ref[0]
-    for tap in range(half):
-        low = coef_ref[tap : tap + 1, :]
-        high = coef_ref[half + tap : half + tap + 1, :]
-        for kind, coef in enumerate((high, low, low + high)):
-            folded[kind, tap * rows : (tap + 1) * rows, :] = (table * coef).astype(jnp.bfloat16)
-
-    @pl.when(step == 0)
-    def _():
-        total[...] = jnp.zeros_like(total)
-
-    for kind in range(3):
-        total[kind] += lax.dot_general(folded[kind], halves[kind], NT, preferred_element_type=jnp.float32)
-
-    @pl.when(step == pl.num_programs(1) - 1)
-    def _():
-        frame = lax.broadcasted_iota(jnp.int32, (rows, LANES), 1) % half
-
-        def shifted_sum(kind, pair):
-            lanes = slice(pair * LANES, (pair + 1) * LANES)
-            both = total[kind, 0:rows, lanes]
-            inside = both
-            for tap in range(1, half):
-                moved = pltpu.roll(total[kind, tap * rows : (tap + 1) * rows, lanes], LANES - tap, 1)
-                both = both + moved
-                inside = inside + jnp.where(frame < half - tap, moved, 0.0)
-            return inside, both - inside
-
-        inside = {}
-        before = {}
-        for pair in range(pairs):
-            (p0, c0), (p1, c1), (p2, c2) = (shifted_sum(kind, pair) for kind in range(3))
-            for place, now, carry in (
-                (2 * pair - 1, p0, c0),
-                (2 * pair, p2 - p0 - p1, c2 - c0 - c1),
-                (2 * pair + 1, p1, c1),
-            ):
-                inside[place] = inside[place] + now if place in inside else now
-                before[place - 1] = before[place - 1] + carry if place - 1 in before else carry
-        count = 2 * pairs
-        channels = rows // 2
-        slots = 4 * count
-        for place in range(-2, count):
-            value = inside.get(place)
-            if place in before:
-                carry = pltpu.roll(before[place], half, 1)
-                value = carry if value is None else value + carry
-            for part in range(2):
-                slot = part * count + place if place >= 0 else (3 + part) * count + place
-                turned[pl.ds(slot, channels, stride=slots), :] = value[part * channels : (part + 1) * channels]
-        nothing = jnp.zeros((channels, LANES), jnp.float32)
+        (p0, c0), (p1, c1), (p2, c2) = (shifted_sum(kind, pair) for kind in range(3))
+        for place, now, carry in (
+            (2 * pair - 1, p0, c0),
+            (2 * pair, p2 - p0 - p1, c2 - c0 - c1),
+            (2 * pair + 1, p1, c1),
+        ):
+            inside[place] = inside[place] + now if place in inside else now
+            before[place - 1] = before[place - 1] + carry if place - 1 in before else carry
+    count = 2 * pairs
+    channels = rows // 2
+    slots = 4 * count
+    for place in range(-2, count):
+        value = inside.get(place)
+        if place in before:
+            carry = pltpu.roll(before[place], half, 1)
+            value = carry if value is None else value + carry
         for part in range(2):
-            for place in range(count - 2):
-                turned[pl.ds((2 + part) * count + place, channels, stride=slots), :] = nothing
-        out_ref[...] = turned[...].astype(jnp.bfloat16).reshape(out_ref.shape)
+            slot = part * count + place if place >= 0 else (3 + part) * count + place
+            turned[pl.ds(slot, channels, stride=slots), :] = value[part * channels : (part + 1) * channels]
+    nothing = jnp.zeros((channels, LANES), jnp.float32)
+    for part in range(2):
+        for place in range(count - 2):
+            turned[pl.ds((2 + part) * count + place, channels, stride=slots), :] = nothing
+    out_ref[...] = turned[...].astype(jnp.bfloat16).reshape(out_ref.shape)
 
 
 def channelize(samples, coefficients, channel_count):
@@ -111,28 +123,27 @@
     columns = inputs * frame_count
     blocks = channel_count // CHANNEL_BLOCK
     slots = 4 * frame_count // half
-    k_block = min(K_BLOCK, frame_len)
+    cuts = (0, frame_len // 4, frame_len)
+    chunks = len(cuts) - 1
     assert inputs * half == LANES and frame_count % taps == 0
     table = jnp.asarray(phase_table(frame_len, channel_count, CH0))
     return pl.pallas_call(
-        functools.partial(channelize_kernel, frame_count),
-        grid=(blocks, frame_len // k_block),
-        in_specs=[
-            pl.BlockSpec((columns, k_block), lambda b, k: (0, k)),
-            pl.BlockSpec((taps, k_block), lambda b, k: (0, k)),
-            pl.BlockSpec((1, rows, k_block), lambda b, k: (b, 0, k)),
-        ],
-        out_specs=pl.BlockSpec((CHANNEL_BLOCK, slots, LANES), lambda b, k: (b, 0, 0)),
+        functools.partial(channelize_kernel, frame_count, cuts),
+        grid=(blocks,),
+        in_specs=[pl.BlockSpec(memory_space=pl.ANY)] * 3,
+        out_specs=pl.BlockSpec((CHANNEL_BLOCK, slots, LANES), lambda b: (b, 0, 0)),
         out_shape=jax.ShapeDtypeStruct((channel_count, slots, LANES), jnp.bfloat16),
         scratch_shapes=[
-            pltpu.VMEM((3, columns // 2, k_block), jnp.bfloat16),
-            pltpu.VMEM((3, half * rows, k_block), jnp.bfloat16),
-            pltpu.VMEM((3, half * rows, columns // 2), jnp.float32),
+            pltpu.VMEM((columns, frame_len), jnp.bfloat16),
+            pltpu.VMEM((taps, frame_len), jnp.float32),
+            pltpu.VMEM((rows, frame_len), jnp.float32),
+            pltpu.VMEM((3, columns // 2, frame_len), jnp.bfloat16),
+            pltpu.VMEM((3, half * rows, frame_len), jnp.bfloat16),
+            pltpu.VMEM((chunks, 3, half * rows, columns // 2), jnp.float32),
             pltpu.VMEM((CHANNEL_BLOCK * slots, LANES), jnp.float32),
+            pltpu.SemaphoreType.DMA((chunks, 3)),
         ],
-        compiler_params=pltpu.CompilerParams(
-            dimension_semantics=("arbitrary", "arbitrary"), vmem_limit_bytes=VMEM_LIMIT
-        ),
+        compiler_params=pltpu.CompilerParams(dimension_semantics=("arbitrary",), vmem_limit_bytes=VMEM_LIMIT),
         cost_estimate=pl.CostEstimate(
             flops=3 * channel_count * taps * columns * frame_len,
             bytes_accessed=2 * columns * frame_len,

time: 32 us -> 29.7 us (0.928)
  Pallas kernels: 16.3 us -> 13.9 us
    pallas_call x1, Pallas kernels: 15.2 us -> 12.8 us  [channelize(): pl.pallas_call(functools.partial(channelize_kernel, frame_count, cuts), g...]
where the time goes in v13:
time: 29.7 us; the launch traced here: 29.5 us
  blocking collectives  15.5 us (52%)
  Pallas kernels  13.9 us (47%)
    all_to_all x1, blocking collectives, on_device(): lax.all_to_all(partial, ('st', 'ta'), split_axis=0, concat_axis=0, tiled=...  15.5 us
    pallas_call x1, Pallas kernels, channelize(): pl.pallas_call(functools.partial(channelize_kernel, frame_count, cuts), g...  12.8 us
    pallas_call x1, Pallas kernels, correlate(): pl.pallas_call(functools.partial(correlate_kernel, half, st_count, ta_cou...  1.11 us

profile of v13, /device:TPU:0, one launch (start us, length us, event | category | flops | bytes accessed | tf_op | source)
XLA Modules:
  0.0 29.5 jit_solution(1014355058321692923)
XLA Ops:
  0.0 12.8 %channelize.1 = bf16[32,16,128]{2,1,0:T(8,128)(2,1)} custom-call(bf16[512,8192]{1,0:T(8,128)(2,1)} %bitcast.1, f32[16,8192]{1,0:T(8,128)} %coef_hbm.1, f32[1,64,8192]{2,1,0:T(8,128)} %constant.2.clone.table_hbm), custom_call_target="tpu_custom_call" | custom-call | flops 6442450944 | bytes 8388608 | tf_op jit(solution)/shard_map/channelize/pallas_call | solution.py:130
  12.8 15.5 %all_to_all.5.in_ref = bf16[32,16,128]{2,1,0:T(8,128)(2,1)S(1)} all-to-all(bf16[32,16,128]{2,1,0:T(8,128)(2,1)} %channelize.1), channel_id=1, replica_groups=mesh['st'=8,'ta'=4] {'st','ta'}, dimensions={0} | all-to-all | bytes 262144 | tf_op jit(solution)/shard_map/all_to_all | solution.py:225
  28.4 1.1 %correlate.1 = bf16[1,2,128,128]{3,2,1,0:T(8,128)(2,1)} custom-call(bf16[32,16,128]{2,1,0:T(8,128)(2,1)S(1)} %all_to_all.5.in_ref), custom_call_target="tpu_custom_call" | custom-call | tf_op jit(solution)/shard_map/correlate/pallas_call | solution.py:205

commit v14 on v10

--- a/solution.py
+++ b/solution.py
@@ -13,7 +13,7 @@
 LANES = 128
 CHANNEL_BLOCK = 32
 K_BLOCK = 2048
-VMEM_LIMIT = 60 * 1024 * 1024
+VMEM_LIMIT = 55000 * 1024
 NT = (((1,), (1,)), ((), ()))
 
 

time: 27.2 us -> 26.4 us (0.971)
  Pallas kernels: 11.5 us -> 10.9 us
    pallas_call x1, Pallas kernels: 10.4 us -> 9.75 us  [channelize(): pl.pallas_call(functools.partial(channelize_kernel, frame_count), grid=(b...]
where the time goes in v14:
time: 26.4 us; the launch traced here: 26.2 us
  blocking collectives  15.3 us (58%)
  Pallas kernels  10.9 us (41%)
    all_to_all x1, blocking collectives, on_device(): lax.all_to_all(partial, ('st', 'ta'), split_axis=0, concat_axis=0, tiled=...  15.3 us
    pallas_call x1, Pallas kernels, channelize(): pl.pallas_call(functools.partial(channelize_kernel, frame_count), grid=(b...  9.75 us
    pallas_call x1, Pallas kernels, correlate(): pl.pallas_call(functools.partial(correlate_kernel, half, st_count, ta_cou...  1.11 us

profile of v14, /device:TPU:0, one launch (start us, length us, event | category | flops | bytes accessed | tf_op | source)
XLA Modules:
  0.0 26.2 jit_solution(9148377047996812078)
XLA Ops:
  0.0 9.7 %channelize.1 = bf16[32,16,128]{2,1,0:T(8,128)(2,1)S(1)} custom-call(bf16[512,8192]{1,0:T(8,128)(2,1)} %bitcast.1, f32[16,8192]{1,0:T(8,128)} %coef_ref.1, f32[1,64,8192]{2,1,0:T(8,128)} %constant.2.clone.table_ref), custom_call_target="tpu_custom_call" | custom-call | flops 6442450944 | bytes 8388608 | tf_op jit(solution)/shard_map/channelize/pallas_call | solution.py:115
  9.8 15.3 %all_to_all.5.in_ref = bf16[32,16,128]{2,1,0:T(8,128)(2,1)S(1)} all-to-all(bf16[32,16,128]{2,1,0:T(8,128)(2,1)S(1)} %channelize.1), channel_id=1, replica_groups=mesh['st'=8,'ta'=4] {'st','ta'}, dimensions={0} | all-to-all | bytes 262144 | tf_op jit(solution)/shard_map/all_to_all | solution.py:212
  25.1 1.1 %correlate.1 = bf16[1,2,128,128]{3,2,1,0:T(8,128)(2,1)} custom-call(bf16[32,16,128]{2,1,0:T(8,128)(2,1)S(1)} %all_to_all.5.in_ref), custom_call_target="tpu_custom_call" | custom-call | tf_op jit(solution)/shard_map/correlate/pallas_call | solution.py:192

commit v15 on v14

--- a/solution.py
+++ b/solution.py
@@ -83,22 +83,20 @@
             ):
                 inside[place] = inside[place] + now if place in inside else now
                 before[place - 1] = before[place - 1] + carry if place - 1 in before else carry
-        count = 2 * pairs
         channels = rows // 2
-        slots = 4 * count
-        for place in range(-2, count):
+        for place in range(-2, 2 * pairs):
             value = inside.get(place)
             if place in before:
                 carry = pltpu.roll(before[place], half, 1)
                 value = carry if value is None else value + carry
             for part in range(2):
-                slot = part * count + place if place >= 0 else (3 + part) * count + place
-                turned[pl.ds(slot, channels, stride=slots), :] = value[part * channels : (part + 1) * channels]
-        nothing = jnp.zeros((channels, LANES), jnp.float32)
-        for part in range(2):
-            for place in range(count - 2):
-                turned[pl.ds((2 + part) * count + place, channels, stride=slots), :] = nothing
-        out_ref[...] = turned[...].astype(jnp.bfloat16).reshape(out_ref.shape)
+                row, column = (place, part) if place >= 0 else (2 * part + place + 2, 2)
+                turned[column, pl.ds(row, channels, stride=2 * pairs), :] = value[part * channels : (part + 1) * channels]
+        for column in range(3):
+            lanes = slice(column * LANES, (column + 1) * LANES)
+            for channel in range(channels):
+                block = turned[column, channel * 2 * pairs : (channel + 1) * 2 * pairs, :]
+                out_ref[channel, :, lanes] = block.astype(jnp.bfloat16)
 
 
 def channelize(samples, coefficients, channel_count):
@@ -108,7 +106,8 @@
     rows = 2 * CHANNEL_BLOCK
     columns = inputs * frame_count
     blocks = channel_count // CHANNEL_BLOCK
-    slots = 4 * frame_count // half
+    slots = frame_count // half
+    assert slots == 4
     k_block = min(K_BLOCK, frame_len)
     assert inputs * half == LANES and frame_count % taps == 0
     table = jnp.asarray(phase_table(frame_len, channel_count, CH0))
@@ -120,13 +119,13 @@
             pl.BlockSpec((taps, k_block), lambda b, k: (0, k)),
             pl.BlockSpec((1, rows, k_block), lambda b, k: (b, 0, k)),
         ],
-        out_specs=pl.BlockSpec((CHANNEL_BLOCK, slots, LANES), lambda b, k: (b, 0, 0)),
-        out_shape=jax.ShapeDtypeStruct((channel_count, slots, LANES), jnp.bfloat16),
+        out_specs=pl.BlockSpec((CHANNEL_BLOCK, slots, 3 * LANES), lambda b, k: (b, 0, 0)),
+        out_shape=jax.ShapeDtypeStruct((channel_count, slots, 3 * LANES), jnp.bfloat16),
         scratch_shapes=[
             pltpu.VMEM((3, columns // 2, k_block), jnp.bfloat16),
             pltpu.VMEM((3, half * rows, k_block), jnp.bfloat16),
             pltpu.VMEM((frame_len // k_block, 3, half * rows, columns // 2), jnp.float32),
-            pltpu.VMEM((CHANNEL_BLOCK * slots, LANES), jnp.float32),
+            pltpu.VMEM((3, CHANNEL_BLOCK * slots, LANES), jnp.float32),
         ],
         compiler_params=pltpu.CompilerParams(
             dimension_semantics=("arbitrary", "arbitrary"), vmem_limit_bytes=VMEM_LIMIT
@@ -141,8 +140,7 @@
 
 
 def correlate_kernel(half, st_count, ta_count, in_ref, out_ref, arranged, across, spectra):
-    slots = in_ref.shape[1] // 2
-    count = slots // 2
+    count = in_ref.shape[1]
     inputs = LANES // half
     places = ta_count * count
     stations = LANES // places
@@ -153,12 +151,14 @@
         for place in range(stations):
             st = group * stations + place
             for ta in range(ta_count):
-                value = in_ref[st * ta_count + ta].astype(jnp.float32)[:slots]
+                row = place * places + ta * count
+                own = in_ref[st * ta_count + ta].astype(jnp.float32)
+                for part in range(2):
+                    arranged[part, row : row + count, :] = own[:, part * LANES : (part + 1) * LANES]
                 if ta < ta_count - 1:
-                    value = value + in_ref[st * ta_count + ta + 1].astype(jnp.float32)[slots:]
-                for part in range(2):
-                    row = place * places + ta * count
-                    arranged[part, row : row + count, :] = value[part * count : (part + 1) * count]
+                    ahead = in_ref[st * ta_count + ta + 1].astype(jnp.float32)[:, 2 * LANES :]
+                    for part in range(2):
+                        arranged[part, row + count - 2 : row + count, :] += ahead[2 * part : 2 * part + 2]
         for part in range(2):
             across[part] = arranged[part].T
             by_frame = [across[part, pl.ds(frame, inputs, stride=half), :] for frame in range(half)]

time: 26.4 us -> 25.9 us (0.981)
  blocking collectives: 15.3 us -> 14.9 us
    all_to_all x1, blocking collectives: 15.3 us -> 14.9 us  [on_device(): lax.all_to_all(partial, ('st', 'ta'), split_axis=0, concat_axis=0, tiled=...]
where the time goes in v15:
time: 25.9 us; the launch traced here: 25.8 us
  blocking collectives  14.9 us (58%)
  Pallas kernels  10.9 us (42%)
    all_to_all x1, blocking collectives, on_device(): lax.all_to_all(partial, ('st', 'ta'), split_axis=0, concat_axis=0, tiled=...  14.9 us
    pallas_call x1, Pallas kernels, channelize(): pl.pallas_call(functools.partial(channelize_kernel, frame_count), grid=(b...  9.73 us
    pallas_call x1, Pallas kernels, correlate(): pl.pallas_call(functools.partial(correlate_kernel, half, st_count, ta_cou...  1.13 us

profile of v15, /device:TPU:0, one launch (start us, length us, event | category | flops | bytes accessed | tf_op | source)
XLA Modules:
  0.0 25.8 jit_solution(2019488313909735270)
XLA Ops:
  0.0 9.7 %channelize.1 = bf16[32,4,384]{2,1,0:T(4,128)(2,1)S(1)} custom-call(bf16[512,8192]{1,0:T(8,128)(2,1)} %bitcast.1, f32[16,8192]{1,0:T(8,128)} %coef_ref.1, f32[1,64,8192]{2,1,0:T(8,128)} %constant.2.clone.table_ref), custom_call_target="tpu_custom_call" | custom-call | flops 6442450944 | bytes 8388608 | tf_op jit(solution)/shard_map/channelize/pallas_call | solution.py:114
  9.7 14.9 %all_to_all.5.in_ref = bf16[32,4,384]{2,1,0:T(4,128)(2,1)S(1)} all-to-all(bf16[32,4,384]{2,1,0:T(4,128)(2,1)S(1)} %channelize.1), channel_id=1, replica_groups=mesh['st'=8,'ta'=4] {'st','ta'}, dimensions={0} | all-to-all | bytes 196608 | tf_op jit(solution)/shard_map/all_to_all | solution.py:212
  24.7 1.1 %correlate.1 = bf16[1,2,128,128]{3,2,1,0:T(8,128)(2,1)} custom-call(bf16[32,4,384]{2,1,0:T(4,128)(2,1)S(1)} %all_to_all.5.in_ref), custom_call_target="tpu_custom_call" | custom-call | tf_op jit(solution)/shard_map/correlate/pallas_call | solution.py:192

commit v16 on v15

--- a/solution.py
+++ b/solution.py
@@ -12,7 +12,7 @@
 CH0 = 1024
 LANES = 128
 CHANNEL_BLOCK = 32
-K_BLOCK = 2048
+K_BLOCK = 4096
 VMEM_LIMIT = 55000 * 1024
 NT = (((1,), (1,)), ((), ()))
 

time: 25.9 us -> 26.3 us (1.015)
  Pallas kernels: 10.9 us -> 11.2 us
    pallas_call x1, Pallas kernels: 9.73 us -> 10 us  [channelize(): pl.pallas_call(functools.partial(channelize_kernel, frame_count), grid=(b...]
where the time goes in v16:
time: 26.3 us; the launch traced here: 26.1 us
  blocking collectives  14.9 us (57%)
  Pallas kernels  11.2 us (43%)
    all_to_all x1, blocking collectives, on_device(): lax.all_to_all(partial, ('st', 'ta'), split_axis=0, concat_axis=0, tiled=...  14.9 us
    pallas_call x1, Pallas kernels, channelize(): pl.pallas_call(functools.partial(channelize_kernel, frame_count), grid=(b...  10 us
    pallas_call x1, Pallas kernels, correlate(): pl.pallas_call(functools.partial(correlate_kernel, half, st_count, ta_cou...  1.12 us

profile of v16, /device:TPU:0, one launch (start us, length us, event | category | flops | bytes accessed | tf_op | source)
XLA Modules:
  0.0 26.1 jit_solution(7805302688543577958)
XLA Ops:
  0.0 10.0 %channelize.1 = bf16[32,4,384]{2,1,0:T(4,128)(2,1)S(1)} custom-call(bf16[512,8192]{1,0:T(8,128)(2,1)} %bitcast.1, f32[16,8192]{1,0:T(8,128)} %coef_ref.1, f32[1,64,8192]{2,1,0:T(8,128)} %constant.2.clone.table_ref), custom_call_target="tpu_custom_call" | custom-call | flops 6442450944 | bytes 8388608 | tf_op jit(solution)/shard_map/channelize/pallas_call | solution.py:114
  10.1 14.9 %all_to_all.5.in_ref = bf16[32,4,384]{2,1,0:T(4,128)(2,1)S(1)} all-to-all(bf16[32,4,384]{2,1,0:T(4,128)(2,1)S(1)} %channelize.1), channel_id=1, replica_groups=mesh['st'=8,'ta'=4] {'st','ta'}, dimensions={0} | all-to-all | bytes 196608 | tf_op jit(solution)/shard_map/all_to_all | solution.py:212
  25.0 1.1 %correlate.1 = bf16[1,2,128,128]{3,2,1,0:T(8,128)(2,1)} custom-call(bf16[32,4,384]{2,1,0:T(4,128)(2,1)S(1)} %all_to_all.5.in_ref), custom_call_target="tpu_custom_call" | custom-call | tf_op jit(solution)/shard_map/correlate/pallas_call | solution.py:192

commit v17 on v13

--- a/solution.py
+++ b/solution.py
@@ -12,7 +12,8 @@
 CH0 = 1024
 LANES = 128
 CHANNEL_BLOCK = 32
-VMEM_LIMIT = 60 * 1024 * 1024
+K_BLOCK = 2048
+VMEM_LIMIT = 55000 * 1024
 NT = (((1,), (1,)), ((), ()))
 
 
@@ -25,49 +26,57 @@
     return blocks.transpose(1, 0, 2, 3).reshape(-1, 2 * CHANNEL_BLOCK, frame_len).astype(np.float32)
 
 
-def channelize_kernel(frame_count, cuts, x_hbm, coef_hbm, table_hbm, out_ref, x_in, coef_in, table_in, halves, folded, total, turned, sems):
+def channelize_kernel(
+    frame_count, x_hbm, coef_hbm, table_hbm, out_ref, x_in, coef_in, table_in, halves, folded, total, turned, sems
+):
     block = pl.program_id(0)
-    taps = coef_hbm.shape[0]
+    chunks, taps, k_block = coef_in.shape
     half = taps // 2
-    rows = table_hbm.shape[1]
+    rows = table_in.shape[1]
     pairs = frame_count // taps
-    inputs = x_hbm.shape[0] // frame_count
-    chunks = [slice(first, last) for first, last in zip(cuts[:-1], cuts[1:])]
-    copies = []
-    for chunk, lanes in enumerate(chunks):
-        copies.append(
-            [
-                pltpu.make_async_copy(coef_hbm.at[:, lanes], coef_in.at[:, lanes], sems.at[chunk, 0]),
-                pltpu.make_async_copy(table_hbm.at[block, :, lanes], table_in.at[:, lanes], sems.at[chunk, 1]),
-                pltpu.make_async_copy(x_hbm.at[:, lanes], x_in.at[:, lanes], sems.at[chunk, 2]),
-            ]
+    inputs = x_in.shape[1] // frame_count
+
+    def copies(chunk):
+        lanes = pl.ds(pl.multiple_of(chunk * k_block, k_block), k_block)
+        return (
+            pltpu.make_async_copy(coef_hbm.at[:, lanes], coef_in.at[chunk], sems.at[0, chunk]),
+            pltpu.make_async_copy(table_hbm.at[block, :, lanes], table_in.at[chunk], sems.at[1, chunk]),
+            pltpu.make_async_copy(x_hbm.at[:, lanes], x_in.at[chunk], sems.at[2, chunk]),
         )
-        for copy in copies[-1]:
+
+    for chunk in range(2):
+        for copy in copies(chunk):
             copy.start()
 
-    for chunk, columns in enumerate(chunks):
-        for copy in copies[chunk]:
+    def multiply(chunk, _):
+        @pl.when(chunk + 2 < chunks)
+        def _():
+            for copy in copies(chunk + 2):
+                copy.start()
+
+        for copy in copies(chunk):
             copy.wait()
-        table = table_in[:, columns]
+        table = table_in[chunk]
         for kind in range(3):
             for pair in range(pairs):
                 for first in range(0, inputs, 2):
                     blocks = []
                     for place in (first, first + 1):
                         row = place * frame_count + pair * taps
-                        blocks.append(x_in[row : row + taps, columns].astype(jnp.float32))
-                    even = jnp.concatenate([block[:half] for block in blocks], 0)
-                    odd = jnp.concatenate([block[half:] for block in blocks], 0)
+                        blocks.append(x_in[chunk, row : row + taps, :].astype(jnp.float32))
+                    even = jnp.concatenate([value[:half] for value in blocks], 0)
+                    odd = jnp.concatenate([value[half:] for value in blocks], 0)
                     row = (pair * inputs + first) * half
-                    halves[kind, row : row + taps, columns] = (even, odd, even + odd)[kind].astype(jnp.bfloat16)
+                    halves[kind, row : row + taps, :] = (even, odd, even + odd)[kind].astype(jnp.bfloat16)
             for tap in range(half):
-                low = coef_in[tap : tap + 1, columns]
-                high = coef_in[half + tap : half + tap + 1, columns]
+                low = coef_in[chunk, tap : tap + 1, :]
+                high = coef_in[chunk, half + tap : half + tap + 1, :]
                 coef = (high, low, low + high)[kind]
-                folded[kind, tap * rows : (tap + 1) * rows, columns] = (table * coef).astype(jnp.bfloat16)
-            total[chunk, kind] = lax.dot_general(
-                folded[kind, :, columns], halves[kind, :, columns], NT, preferred_element_type=jnp.float32
-            )
+                folded[kind, tap * rows : (tap + 1) * rows, :] = (table * coef).astype(jnp.bfloat16)
+            total[chunk, kind] = lax.dot_general(folded[kind], halves[kind], NT, preferred_element_type=jnp.float32)
+        return 0
+
+    lax.fori_loop(0, chunks, multiply, 0)
 
     frame = lax.broadcasted_iota(jnp.int32, (rows, LANES), 1) % half
 
@@ -97,22 +106,20 @@
         ):
             inside[place] = inside[place] + now if place in inside else now
             before[place - 1] = before[place - 1] + carry if place - 1 in before else carry
-    count = 2 * pairs
     channels = rows // 2
-    slots = 4 * count
-    for place in range(-2, count):
+    for place in range(-2, 2 * pairs):
         value = inside.get(place)
         if place in before:
             carry = pltpu.roll(before[place], half, 1)
             value = carry if value is None else value + carry
         for part in range(2):
-            slot = part * count + place if place >= 0 else (3 + part) * count + place
-            turned[pl.ds(slot, channels, stride=slots), :] = value[part * channels : (part + 1) * channels]
-    nothing = jnp.zeros((channels, LANES), jnp.float32)
-    for part in range(2):
-        for place in range(count - 2):
-            turned[pl.ds((2 + part) * count + place, channels, stride=slots), :] = nothing
-    out_ref[...] = turned[...].astype(jnp.bfloat16).reshape(out_ref.shape)
+            row, column = (place, part) if place >= 0 else (2 * part + place + 2, 2)
+            turned[column, pl.ds(row, channels, stride=2 * pairs), :] = value[part * channels : (part + 1) * channels]
+    for column in range(3):
+        lanes = slice(column * LANES, (column + 1) * LANES)
+        for channel in range(channels):
+            block = turned[column, channel * 2 * pairs : (channel + 1) * 2 * pairs, :]
+            out_ref[channel, :, lanes] = block.astype(jnp.bfloat16)
 
 
 def channelize(samples, coefficients, channel_count):
@@ -122,28 +129,31 @@
     rows = 2 * CHANNEL_BLOCK
     columns = inputs * frame_count
     blocks = channel_count // CHANNEL_BLOCK
-    slots = 4 * frame_count // half
-    cuts = (0, frame_len // 4, frame_len)
-    chunks = len(cuts) - 1
+    slots = frame_count // half
+    assert slots == 4
+    k_block = min(K_BLOCK, frame_len // 2)
+    chunks = frame_len // k_block
     assert inputs * half == LANES and frame_count % taps == 0
     table = jnp.asarray(phase_table(frame_len, channel_count, CH0))
     return pl.pallas_call(
-        functools.partial(channelize_kernel, frame_count, cuts),
+        functools.partial(channelize_kernel, frame_count),
         grid=(blocks,),
         in_specs=[pl.BlockSpec(memory_space=pl.ANY)] * 3,
-        out_specs=pl.BlockSpec((CHANNEL_BLOCK, slots, LANES), lambda b: (b, 0, 0)),
-        out_shape=jax.ShapeDtypeStruct((channel_count, slots, LANES), jnp.bfloat16),
+        out_specs=pl.BlockSpec((CHANNEL_BLOCK, slots, 3 * LANES), lambda b: (b, 0, 0)),
+        out_shape=jax.ShapeDtypeStruct((channel_count, slots, 3 * LANES), jnp.bfloat16),
         scratch_shapes=[
-            pltpu.VMEM((columns, frame_len), jnp.bfloat16),
-            pltpu.VMEM((taps, frame_len), jnp.float32),
-            pltpu.VMEM((rows, frame_len), jnp.float32),
-            pltpu.VMEM((3, columns // 2, frame_len), jnp.bfloat16),
-            pltpu.VMEM((3, half * rows, frame_len), jnp.bfloat16),
+            pltpu.VMEM((chunks, columns, k_block), jnp.bfloat16),
+            pltpu.VMEM((chunks, taps, k_block), jnp.float32),
+            pltpu.VMEM((chunks, rows, k_block), jnp.float32),
+            pltpu.VMEM((3, columns // 2, k_block), jnp.bfloat16),
+            pltpu.VMEM((3, half * rows, k_block), jnp.bfloat16),
             pltpu.VMEM((chunks, 3, half * rows, columns // 2), jnp.float32),
-            pltpu.VMEM((CHANNEL_BLOCK * slots, LANES), jnp.float32),
-            pltpu.SemaphoreType.DMA((chunks, 3)),
+            pltpu.VMEM((3, CHANNEL_BLOCK * slots, LANES), jnp.float32),
+            pltpu.SemaphoreType.DMA((3, chunks)),
         ],
-        compiler_params=pltpu.CompilerParams(dimension_semantics=("arbitrary",), vmem_limit_bytes=VMEM_LIMIT),
+        compiler_params=pltpu.CompilerParams(
+            dimension_semantics=("arbitrary",), vmem_limit_bytes=VMEM_LIMIT
+        ),
         cost_estimate=pl.CostEstimate(
             flops=3 * channel_count * taps * columns * frame_len,
             bytes_accessed=2 * columns * frame_len,
@@ -154,8 +164,7 @@
 
 
 def correlate_kernel(half, st_count, ta_count, in_ref, out_ref, arranged, across, spectra):
-    slots = in_ref.shape[1] // 2
-    count = slots // 2
+    count = in_ref.shape[1]
     inputs = LANES // half
     places = ta_count * count
     stations = LANES // places
@@ -166,12 +175,14 @@
         for place in range(stations):
             st = group * stations + place
             for ta in range(ta_count):
-                value = in_ref[st * ta_count + ta].astype(jnp.float32)[:slots]
+                row = place * places + ta * count
+                own = in_ref[st * ta_count + ta].astype(jnp.float32)
+                for part in range(2):
+                    arranged[part, row : row + count, :] = own[:, part * LANES : (part + 1) * LANES]
                 if ta < ta_count - 1:
-                    value = value + in_ref[st * ta_count + ta + 1].astype(jnp.float32)[slots:]
-                for part in range(2):
-                    row = place * places + ta * count
-                    arranged[part, row : row + count, :] = value[part * count : (part + 1) * count]
+                    ahead = in_ref[st * ta_count + ta + 1].astype(jnp.float32)[:, 2 * LANES :]
+                    for part in range(2):
+                        arranged[part, row + count - 2 : row + count, :] += ahead[2 * part : 2 * part + 2]
         for part in range(2):
             across[part] = arranged[part].T
             by_frame = [across[part, pl.ds(frame, inputs, stride=half), :] for frame in range(half)]

time: 29.7 us -> 26.1 us (0.88)
  Pallas kernels: 13.9 us -> 11 us
  blocking collectives: 15.5 us -> 14.9 us
    pallas_call x1, Pallas kernels: 12.8 us -> 9.86 us  [channelize(): pl.pallas_call(functools.partial(channelize_kernel, frame_count), grid=(b...]
    all_to_all x1, blocking collectives: 15.5 us -> 14.9 us  [on_device(): lax.all_to_all(partial, ('st', 'ta'), split_axis=0, concat_axis=0, tiled=...]
where the time goes in v17:
time: 26.1 us; the launch traced here: 25.9 us
  blocking collectives  14.9 us (57%)
  Pallas kernels  11 us (42%)
    all_to_all x1, blocking collectives, on_device(): lax.all_to_all(partial, ('st', 'ta'), split_axis=0, concat_axis=0, tiled=...  14.9 us
    pallas_call x1, Pallas kernels, channelize(): pl.pallas_call(functools.partial(channelize_kernel, frame_count), grid=(b...  9.86 us
    pallas_call x1, Pallas kernels, correlate(): pl.pallas_call(functools.partial(correlate_kernel, half, st_count, ta_cou...  1.13 us

profile of v17, /device:TPU:0, one launch (start us, length us, event | category | flops | bytes accessed | tf_op | source)
XLA Modules:
  0.0 25.9 jit_solution(10928541296503228028)
XLA Ops:
  0.0 9.9 %channelize.1 = bf16[32,4,384]{2,1,0:T(4,128)(2,1)S(1)} custom-call(bf16[512,8192]{1,0:T(8,128)(2,1)} %bitcast.1, f32[16,8192]{1,0:T(8,128)} %coef_hbm.1, f32[1,64,8192]{2,1,0:T(8,128)} %constant.2.clone.table_hbm), custom_call_target="tpu_custom_call" | custom-call | flops 6442450944 | bytes 8388608 | tf_op jit(solution)/shard_map/channelize/pallas_call | solution.py:138
  9.9 14.9 %all_to_all.5.in_ref = bf16[32,4,384]{2,1,0:T(4,128)(2,1)S(1)} all-to-all(bf16[32,4,384]{2,1,0:T(4,128)(2,1)S(1)} %channelize.1), channel_id=1, replica_groups=mesh['st'=8,'ta'=4] {'st','ta'}, dimensions={0} | all-to-all | bytes 196608 | tf_op jit(solution)/shard_map/all_to_all | solution.py:236
  24.8 1.1 %correlate.1 = bf16[1,2,128,128]{3,2,1,0:T(8,128)(2,1)} custom-call(bf16[32,4,384]{2,1,0:T(4,128)(2,1)S(1)} %all_to_all.5.in_ref), custom_call_target="tpu_custom_call" | custom-call | tf_op jit(solution)/shard_map/correlate/pallas_call | solution.py:216

commit v18 on v17

--- a/solution.py
+++ b/solution.py
@@ -27,7 +27,7 @@
 
 
 def channelize_kernel(
-    frame_count, x_hbm, coef_hbm, table_hbm, out_ref, x_in, coef_in, table_in, halves, folded, total, turned, sems
+    frame_count, x_hbm, coef_hbm, table_hbm, out_ref, x_in, coef_in, table_in, halves, folded, halves_odd, folded_odd, total, turned, sems
 ):
     block = pl.program_id(0)
     chunks, taps, k_block = coef_in.shape
@@ -44,18 +44,15 @@
             pltpu.make_async_copy(x_hbm.at[:, lanes], x_in.at[chunk], sems.at[2, chunk]),
         )
 
-    for chunk in range(2):
+    def start(chunk):
         for copy in copies(chunk):
             copy.start()
 
-    def multiply(chunk, _):
-        @pl.when(chunk + 2 < chunks)
-        def _():
-            for copy in copies(chunk + 2):
-                copy.start()
-
+    def wait(chunk):
         for copy in copies(chunk):
             copy.wait()
+
+    def form(chunk, halves, folded):
         table = table_in[chunk]
         for kind in range(3):
             for pair in range(pairs):
@@ -73,10 +70,37 @@
                 high = coef_in[chunk, half + tap : half + tap + 1, :]
                 coef = (high, low, low + high)[kind]
                 folded[kind, tap * rows : (tap + 1) * rows, :] = (table * coef).astype(jnp.bfloat16)
+
+    def multiply(chunk, halves, folded):
+        for kind in range(3):
             total[chunk, kind] = lax.dot_general(folded[kind], halves[kind], NT, preferred_element_type=jnp.float32)
+
+    start(0)
+    start(1)
+    wait(0)
+    form(0, halves, folded)
+
+    def two_chunks(turn, _):
+        chunk = 2 * turn
+
+        @pl.when(chunk + 2 < chunks)
+        def _():
+            start(chunk + 2)
+            start(chunk + 3)
+
+        wait(chunk + 1)
+        multiply(chunk, halves, folded)
+        form(chunk + 1, halves_odd, folded_odd)
+
+        @pl.when(chunk + 2 < chunks)
+        def _():
+            wait(chunk + 2)
+
+        multiply(chunk + 1, halves_odd, folded_odd)
+        form(jnp.minimum(chunk + 2, chunks - 1), halves, folded)
         return 0
 
-    lax.fori_loop(0, chunks, multiply, 0)
+    lax.fori_loop(0, chunks // 2, two_chunks, 0)
 
     frame = lax.broadcasted_iota(jnp.int32, (rows, LANES), 1) % half
 
@@ -133,6 +157,7 @@
     assert slots == 4
     k_block = min(K_BLOCK, frame_len // 2)
     chunks = frame_len // k_block
+    assert chunks % 2 == 0
     assert inputs * half == LANES and frame_count % taps == 0
     table = jnp.asarray(phase_table(frame_len, channel_count, CH0))
     return pl.pallas_call(
@@ -145,6 +170,8 @@
             pltpu.VMEM((chunks, columns, k_block), jnp.bfloat16),
             pltpu.VMEM((chunks, taps, k_block), jnp.float32),
             pltpu.VMEM((chunks, rows, k_block), jnp.float32),
+            pltpu.VMEM((3, columns // 2, k_block), jnp.bfloat16),
+            pltpu.VMEM((3, half * rows, k_block), jnp.bfloat16),
             pltpu.VMEM((3, columns // 2, k_block), jnp.bfloat16),
             pltpu.VMEM((3, half * rows, k_block), jnp.bfloat16),
             pltpu.VMEM((chunks, 3, half * rows, columns // 2), jnp.float32),

time: 26.1 us -> 36.1 us (1.38)
  Pallas kernels: 11 us -> 21.1 us
    pallas_call x1, Pallas kernels: 9.86 us -> 19.9 us  [channelize(): pl.pallas_call(functools.partial(channelize_kernel, frame_count), grid=(b...]
where the time goes in v18:
time: 36.1 us; the launch traced here: 36 us
  Pallas kernels  21.1 us (58%)
  blocking collectives  14.9 us (41%)
    pallas_call x1, Pallas kernels, channelize(): pl.pallas_call(functools.partial(channelize_kernel, frame_count), grid=(b...  19.9 us
    all_to_all x1, blocking collectives, on_device(): lax.all_to_all(partial, ('st', 'ta'), split_axis=0, concat_axis=0, tiled=...  14.9 us
    pallas_call x1, Pallas kernels, correlate(): pl.pallas_call(functools.partial(correlate_kernel, half, st_count, ta_cou...  1.13 us

profile of v18, /device:TPU:0, one launch (start us, length us, event | category | flops | bytes accessed | tf_op | source)
XLA Modules:
  0.0 36.0 jit_solution(7049122063544273194)
XLA Ops:
  0.0 19.9 %channelize.1 = bf16[32,4,384]{2,1,0:T(4,128)(2,1)S(1)} custom-call(bf16[512,8192]{1,0:T(8,128)(2,1)} %bitcast.1, f32[16,8192]{1,0:T(8,128)} %coef_hbm.1, f32[1,64,8192]{2,1,0:T(8,128)} %constant.2.clone.table_hbm), custom_call_target="tpu_custom_call" | custom-call | flops 6442450944 | bytes 8388608 | tf_op jit(solution)/shard_map/channelize/pallas_call | solution.py:163
  19.9 14.9 %all_to_all.5.in_ref = bf16[32,4,384]{2,1,0:T(4,128)(2,1)S(1)} all-to-all(bf16[32,4,384]{2,1,0:T(4,128)(2,1)S(1)} %channelize.1), channel_id=1, replica_groups=mesh['st'=8,'ta'=4] {'st','ta'}, dimensions={0} | all-to-all | bytes 196608 | tf_op jit(solution)/shard_map/all_to_all | solution.py:263
  34.9 1.1 %correlate.1 = bf16[1,2,128,128]{3,2,1,0:T(8,128)(2,1)} custom-call(bf16[32,4,384]{2,1,0:T(4,128)(2,1)S(1)} %all_to_all.5.in_ref), custom_call_target="tpu_custom_call" | custom-call | tf_op jit(solution)/shard_map/correlate/pallas_call | solution.py:243

commit v19 on v15

--- a/solution.py
+++ b/solution.py
@@ -35,17 +35,19 @@
     inputs = x_ref.shape[0] // frame_count
 
     table = table_ref[0]
+    for pair in range(pairs):
+        for first in range(0, inputs, 2):
+            top, bottom = [
+                x_ref[place * frame_count + pair * taps : place * frame_count + (pair + 1) * taps, :]
+                for place in (first, first + 1)
+            ]
+            even = jnp.concatenate([top[:half], bottom[:half]], 0)
+            odd = jnp.concatenate([top[half:], bottom[half:]], 0)
+            row = (pair * inputs + first) * half
+            halves[0, row : row + taps, :] = even
+            halves[1, row : row + taps, :] = odd
+            halves[2, row : row + taps, :] = even + odd
     for kind in range(3):
-        for pair in range(pairs):
-            for first in range(0, inputs, 2):
-                blocks = []
-                for place in (first, first + 1):
-                    row = place * frame_count + pair * taps
-                    blocks.append(x_ref[row : row + taps, :].astype(jnp.float32))
-                even = jnp.concatenate([block[:half] for block in blocks], 0)
-                odd = jnp.concatenate([block[half:] for block in blocks], 0)
-                row = (pair * inputs + first) * half
-                halves[kind, row : row + taps, :] = (even, odd, even + odd)[kind].astype(jnp.bfloat16)
         for tap in range(half):
             low = coef_ref[tap : tap + 1, :]
             high = coef_ref[half + tap : half + tap + 1, :]

time: 25.9 us -> 26 us (level)
  no operation moved by 1% of the time
where the time goes in v19:
time: 26 us; the launch traced here: 25.8 us
  blocking collectives  14.9 us (57%)
  Pallas kernels  10.9 us (42%)
    all_to_all x1, blocking collectives, on_device(): lax.all_to_all(partial, ('st', 'ta'), split_axis=0, concat_axis=0, tiled=...  14.9 us
    pallas_call x1, Pallas kernels, channelize(): pl.pallas_call(functools.partial(channelize_kernel, frame_count), grid=(b...  9.76 us
    pallas_call x1, Pallas kernels, correlate(): pl.pallas_call(functools.partial(correlate_kernel, half, st_count, ta_cou...  1.13 us

profile of v19, /device:TPU:0, one launch (start us, length us, event | category | flops | bytes accessed | tf_op | source)
XLA Modules:
  0.0 25.8 jit_solution(16466223933602778326)
XLA Ops:
  0.0 9.8 %channelize.1 = bf16[32,4,384]{2,1,0:T(4,128)(2,1)S(1)} custom-call(bf16[512,8192]{1,0:T(8,128)(2,1)} %bitcast.1, f32[16,8192]{1,0:T(8,128)} %coef_ref.1, f32[1,64,8192]{2,1,0:T(8,128)} %constant.2.clone.table_ref), custom_call_target="tpu_custom_call" | custom-call | flops 6442450944 | bytes 8388608 | tf_op jit(solution)/shard_map/channelize/pallas_call | solution.py:116
  9.8 14.9 %all_to_all.5.in_ref = bf16[32,4,384]{2,1,0:T(4,128)(2,1)S(1)} all-to-all(bf16[32,4,384]{2,1,0:T(4,128)(2,1)S(1)} %channelize.1), channel_id=1, replica_groups=mesh['st'=8,'ta'=4] {'st','ta'}, dimensions={0} | all-to-all | bytes 196608 | tf_op jit(solution)/shard_map/all_to_all | solution.py:214
  24.7 1.1 %correlate.1 = bf16[1,2,128,128]{3,2,1,0:T(8,128)(2,1)} custom-call(bf16[32,4,384]{2,1,0:T(4,128)(2,1)S(1)} %all_to_all.5.in_ref), custom_call_target="tpu_custom_call" | custom-call | tf_op jit(solution)/shard_map/correlate/pallas_call | solution.py:194

commit v20 on v19

--- a/solution.py
+++ b/solution.py
@@ -142,27 +142,30 @@
 
 
 def correlate_kernel(half, st_count, ta_count, in_ref, out_ref, arranged, across, spectra):
-    count = in_ref.shape[1]
+    sources, count, _ = in_ref.shape
     inputs = LANES // half
     places = ta_count * count
     stations = LANES // places
     all_inputs = st_count * inputs
     position = lax.broadcasted_iota(jnp.int32, (inputs, LANES), 1) // places
 
+    def plane(column):
+        lanes = slice(column * LANES, (column + 1) * LANES)
+        return in_ref[:, :, lanes].astype(jnp.float32).reshape(sources * count, LANES)
+
+    row = lax.broadcasted_iota(jnp.int32, (sources * count, LANES), 0)
+    takes = (row % count >= count - 2) & (row % places < places - count)
+    ahead = plane(2)
+    for part in range(2):
+        moved = pltpu.roll(ahead, sources * count - (2 + 2 * part), 0)
+        arranged[part] = plane(part) + jnp.where(takes, moved, 0.0)
+
     def station_group(group):
-        for place in range(stations):
-            st = group * stations + place
-            for ta in range(ta_count):
-                row = place * places + ta * count
-                own = in_ref[st * ta_count + ta].astype(jnp.float32)
-                for part in range(2):
-                    arranged[part, row : row + count, :] = own[:, part * LANES : (part + 1) * LANES]
-                if ta < ta_count - 1:
-                    ahead = in_ref[st * ta_count + ta + 1].astype(jnp.float32)[:, 2 * LANES :]
-                    for part in range(2):
-                        arranged[part, row + count - 2 : row + count, :] += ahead[2 * part : 2 * part + 2]
         for part in range(2):
-            across[part] = arranged[part].T
+            first = group * LANES
+            if not isinstance(first, int):
+                first = pl.multiple_of(first, LANES)
+            across[part] = arranged[part, pl.ds(first, LANES), :].T
             by_frame = [across[part, pl.ds(frame, inputs, stride=half), :] for frame in range(half)]
             for place in range(stations):
                 result = None
@@ -170,17 +173,17 @@
                     shift = ((frame - place) * places) % LANES
                     value = pltpu.roll(by_frame[frame], shift, 1) if shift else by_frame[frame]
                     result = value if result is None else jnp.where(position == frame, value, result)
-                first = part * all_inputs + (group * stations + place) * inputs
+                first = (group * stations + place) * inputs
                 if not isinstance(first, int):
                     first = pl.multiple_of(first, inputs)
-                spectra[pl.ds(first, inputs), :] = result
+                spectra[part, pl.ds(first, inputs), :] = result
 
     if st_count == stations:
         station_group(0)
     else:
         lax.fori_loop(0, st_count // stations, lambda group, _: (station_group(group), 0)[1], 0)
-    real_part = spectra[:all_inputs, :].astype(jnp.bfloat16)
-    imag_part = spectra[all_inputs:, :].astype(jnp.bfloat16)
+    real_part = spectra[0].astype(jnp.bfloat16)
+    imag_part = spectra[1].astype(jnp.bfloat16)
     right = jnp.concatenate([real_part, imag_part], 1)
     left = jnp.concatenate([imag_part, -real_part], 1)
     scale = 1.0 / LANES
@@ -197,9 +200,9 @@
         out_specs=pl.BlockSpec(memory_space=pltpu.VMEM),
         out_shape=jax.ShapeDtypeStruct((1, 2, all_inputs, all_inputs), jnp.bfloat16),
         scratch_shapes=[
+            pltpu.VMEM((2, arrived.shape[0] * arrived.shape[1], LANES), jnp.float32),
             pltpu.VMEM((2, LANES, LANES), jnp.float32),
-            pltpu.VMEM((2, LANES, LANES), jnp.float32),
-            pltpu.VMEM((2 * all_inputs, LANES), jnp.float32),
+            pltpu.VMEM((2, all_inputs, LANES), jnp.float32),
         ],
         compiler_params=pltpu.CompilerParams(vmem_limit_bytes=32 * 1024 * 1024),
         name="correlate",

time: 26 us -> 26 us (level)
  no operation moved by 1% of the time
where the time goes in v20:
time: 26 us; the launch traced here: 25.8 us
  blocking collectives  14.9 us (57%)
  Pallas kernels  10.9 us (42%)
    all_to_all x1, blocking collectives, on_device(): lax.all_to_all(partial, ('st', 'ta'), split_axis=0, concat_axis=0, tiled=...  14.9 us
    pallas_call x1, Pallas kernels, channelize(): pl.pallas_call(functools.partial(channelize_kernel, frame_count), grid=(b...  9.76 us
    pallas_call x1, Pallas kernels, correlate(): pl.pallas_call(functools.partial(correlate_kernel, half, st_count, ta_cou...  1.12 us

profile of v20, /device:TPU:0, one launch (start us, length us, event | category | flops | bytes accessed | tf_op | source)
XLA Modules:
  0.0 25.8 jit_solution(16460165531421982148)
XLA Ops:
  0.0 9.8 %channelize.1 = bf16[32,4,384]{2,1,0:T(4,128)(2,1)S(1)} custom-call(bf16[512,8192]{1,0:T(8,128)(2,1)} %bitcast.1, f32[16,8192]{1,0:T(8,128)} %coef_ref.1, f32[1,64,8192]{2,1,0:T(8,128)} %constant.2.clone.table_ref), custom_call_target="tpu_custom_call" | custom-call | flops 6442450944 | bytes 8388608 | tf_op jit(solution)/shard_map/channelize/pallas_call | solution.py:116
  9.8 14.9 %all_to_all.5.in_ref = bf16[32,4,384]{2,1,0:T(4,128)(2,1)S(1)} all-to-all(bf16[32,4,384]{2,1,0:T(4,128)(2,1)S(1)} %channelize.1), channel_id=1, replica_groups=mesh['st'=8,'ta'=4] {'st','ta'}, dimensions={0} | all-to-all | bytes 196608 | tf_op jit(solution)/shard_map/all_to_all | solution.py:217
  24.7 1.1 %correlate.1 = bf16[1,2,128,128]{3,2,1,0:T(8,128)(2,1)} custom-call(bf16[32,4,384]{2,1,0:T(4,128)(2,1)S(1)} %all_to_all.5.in_ref), custom_call_target="tpu_custom_call" | custom-call | tf_op jit(solution)/shard_map/correlate/pallas_call | solution.py:197

commit v21 on v19

--- a/solution.py
+++ b/solution.py
@@ -26,7 +26,7 @@
     return blocks.transpose(1, 0, 2, 3).reshape(-1, 2 * CHANNEL_BLOCK, frame_len).astype(np.float32)
 
 
-def channelize_kernel(frame_count, x_ref, coef_ref, table_ref, out_ref, halves, folded, total, turned):
+def channelize_kernel(frame_count, x_ref, coef_ref, table_ref, out_ref, halves, folded, total, sums, turned):
     step = pl.program_id(1)
     taps = coef_ref.shape[0]
     half = taps // 2
@@ -59,25 +59,29 @@
     def _():
         frame = lax.broadcasted_iota(jnp.int32, (rows, LANES), 1) % half
 
-        def shifted_sum(kind, pair):
-            lanes = slice(pair * LANES, (pair + 1) * LANES)
+        def shifted_sum(index, _):
+            kind, pair = index // pairs, index % pairs
+            lanes = pl.ds(pl.multiple_of(pair * LANES, LANES), LANES)
 
             def summed(tap):
                 slots = [total[chunk, kind, tap * rows : (tap + 1) * rows, lanes] for chunk in range(total.shape[0])]
                 return functools.reduce(jnp.add, slots)
 
             both = summed(0)
-            inside = both
+            within = both
             for tap in range(1, half):
                 moved = pltpu.roll(summed(tap), LANES - tap, 1)
                 both = both + moved
-                inside = inside + jnp.where(frame < half - tap, moved, 0.0)
-            return inside, both - inside
-
+                within = within + jnp.where(frame < half - tap, moved, 0.0)
+            sums[index, 0] = within
+            sums[index, 1] = both - within
+            return 0
+
+        lax.fori_loop(0, 3 * pairs, shifted_sum, 0)
         inside = {}
         before = {}
         for pair in range(pairs):
-            (p0, c0), (p1, c1), (p2, c2) = (shifted_sum(kind, pair) for kind in range(3))
+            (p0, c0), (p1, c1), (p2, c2) = ((sums[kind * pairs + pair, 0], sums[kind * pairs + pair, 1]) for kind in range(3))
             for place, now, carry in (
                 (2 * pair - 1, p0, c0),
                 (2 * pair, p2 - p0 - p1, c2 - c0 - c1),
@@ -127,6 +131,7 @@
             pltpu.VMEM((3, columns // 2, k_block), jnp.bfloat16),
             pltpu.VMEM((3, half * rows, k_block), jnp.bfloat16),
             pltpu.VMEM((frame_len // k_block, 3, half * rows, columns // 2), jnp.float32),
+            pltpu.VMEM((3 * frame_count // taps, 2, rows, LANES), jnp.float32),
             pltpu.VMEM((3, CHANNEL_BLOCK * slots, LANES), jnp.float32),
         ],
         compiler_params=pltpu.CompilerParams(

time: 26 us -> 26.3 us (1.012)
  Pallas kernels: 10.9 us -> 11.3 us
    pallas_call x1, Pallas kernels: 9.76 us -> 10.1 us  [channelize(): pl.pallas_call(functools.partial(channelize_kernel, frame_count), grid=(b...]
where the time goes in v21:
time: 26.3 us; the launch traced here: 26.2 us
  blocking collectives  14.9 us (57%)
  Pallas kernels  11.3 us (43%)
    all_to_all x1, blocking collectives, on_device(): lax.all_to_all(partial, ('st', 'ta'), split_axis=0, concat_axis=0, tiled=...  14.9 us
    pallas_call x1, Pallas kernels, channelize(): pl.pallas_call(functools.partial(channelize_kernel, frame_count), grid=(b...  10.1 us
    pallas_call x1, Pallas kernels, correlate(): pl.pallas_call(functools.partial(correlate_kernel, half, st_count, ta_cou...  1.13 us

profile of v21, /device:TPU:0, one launch (start us, length us, event | category | flops | bytes accessed | tf_op | source)
XLA Modules:
  0.0 26.2 jit_solution(711045946381634873)
XLA Ops:
  0.0 10.1 %channelize.1 = bf16[32,4,384]{2,1,0:T(4,128)(2,1)S(1)} custom-call(bf16[512,8192]{1,0:T(8,128)(2,1)} %bitcast.1, f32[16,8192]{1,0:T(8,128)} %coef_ref.1, f32[1,64,8192]{2,1,0:T(8,128)} %constant.2.clone.table_ref), custom_call_target="tpu_custom_call" | custom-call | flops 6442450944 | bytes 8388608 | tf_op jit(solution)/shard_map/channelize/pallas_call | solution.py:120
  10.1 14.9 %all_to_all.5.in_ref = bf16[32,4,384]{2,1,0:T(4,128)(2,1)S(1)} all-to-all(bf16[32,4,384]{2,1,0:T(4,128)(2,1)S(1)} %channelize.1), channel_id=1, replica_groups=mesh['st'=8,'ta'=4] {'st','ta'}, dimensions={0} | all-to-all | bytes 196608 | tf_op jit(solution)/shard_map/all_to_all | solution.py:219
  25.1 1.1 %correlate.1 = bf16[1,2,128,128]{3,2,1,0:T(8,128)(2,1)} custom-call(bf16[32,4,384]{2,1,0:T(4,128)(2,1)S(1)} %all_to_all.5.in_ref), custom_call_target="tpu_custom_call" | custom-call | tf_op jit(solution)/shard_map/correlate/pallas_call | solution.py:199

commit v22 on v19

--- a/solution.py
+++ b/solution.py
@@ -13,6 +13,7 @@
 LANES = 128
 CHANNEL_BLOCK = 32
 K_BLOCK = 2048
+ROW_GROUP = 16
 VMEM_LIMIT = 55000 * 1024
 NT = (((1,), (1,)), ((), ()))
 
@@ -57,47 +58,47 @@
 
     @pl.when(step == pl.num_programs(1) - 1)
     def _():
-        frame = lax.broadcasted_iota(jnp.int32, (rows, LANES), 1) % half
-
-        def shifted_sum(kind, pair):
-            lanes = slice(pair * LANES, (pair + 1) * LANES)
-
-            def summed(tap):
-                slots = [total[chunk, kind, tap * rows : (tap + 1) * rows, lanes] for chunk in range(total.shape[0])]
-                return functools.reduce(jnp.add, slots)
-
-            both = summed(0)
-            inside = both
-            for tap in range(1, half):
-                moved = pltpu.roll(summed(tap), LANES - tap, 1)
-                both = both + moved
-                inside = inside + jnp.where(frame < half - tap, moved, 0.0)
-            return inside, both - inside
-
-        inside = {}
-        before = {}
-        for pair in range(pairs):
-            (p0, c0), (p1, c1), (p2, c2) = (shifted_sum(kind, pair) for kind in range(3))
-            for place, now, carry in (
-                (2 * pair - 1, p0, c0),
-                (2 * pair, p2 - p0 - p1, c2 - c0 - c1),
-                (2 * pair + 1, p1, c1),
-            ):
-                inside[place] = inside[place] + now if place in inside else now
-                before[place - 1] = before[place - 1] + carry if place - 1 in before else carry
         channels = rows // 2
-        for place in range(-2, 2 * pairs):
-            value = inside.get(place)
-            if place in before:
-                carry = pltpu.roll(before[place], half, 1)
-                value = carry if value is None else value + carry
-            for part in range(2):
+        count = 2 * pairs
+        frame = lax.broadcasted_iota(jnp.int32, (ROW_GROUP, LANES), 1) % half
+        for group in range(0, rows, ROW_GROUP):
+            part, channel = group // channels, group % channels
+
+            def summed(kind, pair, tap):
+                rows_of = slice(tap * rows + group, tap * rows + group + ROW_GROUP)
+                lanes = slice(pair * LANES, (pair + 1) * LANES)
+                return functools.reduce(jnp.add, [total[c, kind, rows_of, lanes] for c in range(total.shape[0])])
+
+            inside = {}
+            outside = {}
+            for tap in range(half):
+                at = {}
+                for pair in range(pairs):
+                    high, low, mixed = (summed(kind, pair, tap) for kind in range(3))
+                    before = 2 * pair - 1
+                    at[before] = at[before] + high if before in at else high
+                    at[2 * pair] = mixed - high - low
+                    at[2 * pair + 1] = low
+                for place, value in at.items():
+                    if tap == 0:
+                        inside[place] = value
+                        continue
+                    moved = pltpu.roll(value, LANES - tap, 1)
+                    stays = frame < half - tap
+                    inside[place] = inside[place] + jnp.where(stays, moved, 0.0)
+                    leaves = jnp.where(stays, 0.0, moved)
+                    outside[place] = outside[place] + leaves if place in outside else leaves
+            for place in range(-2, count):
+                value = inside.get(place)
+                if place + 1 in outside:
+                    carry = pltpu.roll(outside[place + 1], half, 1)
+                    value = carry if value is None else value + carry
                 row, column = (place, part) if place >= 0 else (2 * part + place + 2, 2)
-                turned[column, pl.ds(row, channels, stride=2 * pairs), :] = value[part * channels : (part + 1) * channels]
+                turned[column, pl.ds(channel * count + row, ROW_GROUP, stride=count), :] = value
         for column in range(3):
             lanes = slice(column * LANES, (column + 1) * LANES)
             for channel in range(channels):
-                block = turned[column, channel * 2 * pairs : (channel + 1) * 2 * pairs, :]
+                block = turned[column, channel * count : (channel + 1) * count, :]
                 out_ref[channel, :, lanes] = block.astype(jnp.bfloat16)
 
 

time: 26 us -> 26 us (level)
  no operation moved by 1% of the time
where the time goes in v22:
time: 26 us; the launch traced here: 25.9 us
  blocking collectives  14.9 us (57%)
  Pallas kernels  11 us (42%)
    all_to_all x1, blocking collectives, on_device(): lax.all_to_all(partial, ('st', 'ta'), split_axis=0, concat_axis=0, tiled=...  14.9 us
    pallas_call x1, Pallas kernels, channelize(): pl.pallas_call(functools.partial(channelize_kernel, frame_count), grid=(b...  9.83 us
    pallas_call x1, Pallas kernels, correlate(): pl.pallas_call(functools.partial(correlate_kernel, half, st_count, ta_cou...  1.12 us

profile of v22, /device:TPU:0, one launch (start us, length us, event | category | flops | bytes accessed | tf_op | source)
XLA Modules:
  0.0 25.9 jit_solution(16734817379127347618)
XLA Ops:
  0.0 9.8 %channelize.1 = bf16[32,4,384]{2,1,0:T(4,128)(2,1)S(1)} custom-call(bf16[512,8192]{1,0:T(8,128)(2,1)} %bitcast.1, f32[16,8192]{1,0:T(8,128)} %coef_ref.1, f32[1,64,8192]{2,1,0:T(8,128)} %constant.2.clone.table_ref), custom_call_target="tpu_custom_call" | custom-call | flops 6442450944 | bytes 8388608 | tf_op jit(solution)/shard_map/channelize/pallas_call | solution.py:117
  9.8 14.9 %all_to_all.5.in_ref = bf16[32,4,384]{2,1,0:T(4,128)(2,1)S(1)} all-to-all(bf16[32,4,384]{2,1,0:T(4,128)(2,1)S(1)} %channelize.1), channel_id=1, replica_groups=mesh['st'=8,'ta'=4] {'st','ta'}, dimensions={0} | all-to-all | bytes 196608 | tf_op jit(solution)/shard_map/all_to_all | solution.py:215
  24.8 1.1 %correlate.1 = bf16[1,2,128,128]{3,2,1,0:T(8,128)(2,1)} custom-call(bf16[32,4,384]{2,1,0:T(4,128)(2,1)S(1)} %all_to_all.5.in_ref), custom_call_target="tpu_custom_call" | custom-call | tf_op jit(solution)/shard_map/correlate/pallas_call | solution.py:195

commit v23 on v19

--- a/solution.py
+++ b/solution.py
@@ -96,9 +96,7 @@
                 turned[column, pl.ds(row, channels, stride=2 * pairs), :] = value[part * channels : (part + 1) * channels]
         for column in range(3):
             lanes = slice(column * LANES, (column + 1) * LANES)
-            for channel in range(channels):
-                block = turned[column, channel * 2 * pairs : (channel + 1) * 2 * pairs, :]
-                out_ref[channel, :, lanes] = block.astype(jnp.bfloat16)
+            out_ref[:, :, lanes] = turned[column].reshape(channels, 2 * pairs, LANES).astype(jnp.bfloat16)
 
 
 def channelize(samples, coefficients, channel_count):

time: 26 us -> 26 us (level)
  no operation moved by 1% of the time
where the time goes in v23:
time: 26 us; the launch traced here: 25.8 us
  blocking collectives  14.9 us (57%)
  Pallas kernels  10.9 us (42%)
    all_to_all x1, blocking collectives, on_device(): lax.all_to_all(partial, ('st', 'ta'), split_axis=0, concat_axis=0, tiled=...  14.9 us
    pallas_call x1, Pallas kernels, channelize(): pl.pallas_call(functools.partial(channelize_kernel, frame_count), grid=(b...  9.76 us
    pallas_call x1, Pallas kernels, correlate(): pl.pallas_call(functools.partial(correlate_kernel, half, st_count, ta_cou...  1.12 us

profile of v23, /device:TPU:0, one launch (start us, length us, event | category | flops | bytes accessed | tf_op | source)
XLA Modules:
  0.0 25.8 jit_solution(13236334346914481783)
XLA Ops:
  0.0 9.8 %channelize.1 = bf16[32,4,384]{2,1,0:T(4,128)(2,1)S(1)} custom-call(bf16[512,8192]{1,0:T(8,128)(2,1)} %bitcast.1, f32[16,8192]{1,0:T(8,128)} %coef_ref.1, f32[1,64,8192]{2,1,0:T(8,128)} %constant.2.clone.table_ref), custom_call_target="tpu_custom_call" | custom-call | flops 6442450944 | bytes 8388608 | tf_op jit(solution)/shard_map/channelize/pallas_call | solution.py:114
  9.8 14.9 %all_to_all.5.in_ref = bf16[32,4,384]{2,1,0:T(4,128)(2,1)S(1)} all-to-all(bf16[32,4,384]{2,1,0:T(4,128)(2,1)S(1)} %channelize.1), channel_id=1, replica_groups=mesh['st'=8,'ta'=4] {'st','ta'}, dimensions={0} | all-to-all | bytes 196608 | tf_op jit(solution)/shard_map/all_to_all | solution.py:212
  24.7 1.1 %correlate.1 = bf16[1,2,128,128]{3,2,1,0:T(8,128)(2,1)} custom-call(bf16[32,4,384]{2,1,0:T(4,128)(2,1)S(1)} %all_to_all.5.in_ref), custom_call_target="tpu_custom_call" | custom-call | tf_op jit(solution)/shard_map/correlate/pallas_call | solution.py:192
